TPU v7x, 128 devices: a whole 4x4x4 slice. The times are simulated.
128 devices in a mesh: row: 32 (over x, z, y_lo), col: 4 (over y_hi, core).
Axes of the slice: x: 4, y: 4 (y_hi: 2, y_lo: 2; y = y_hi * 2 + y_lo), z: 4, core: 2. Of those that a mesh axis runs over, the one named last changes fastest.
Arguments:
- contrib: float32 [2, 8192, 8192], P(None, 'row', 'col'), may hold values from -4 to 4
- target_rows: int32 [2, 8192], P(None, 'row'), may hold values from 0 to 8191, as said below
- diag_shift: float32 [2, 1, 32, 256], P(None, None, 'row'), may hold values from 300 to 600
- pattern: int32 [2, 32], replicated, may hold values 0 or 1
Outputs:
- factored: float32 [2, 1, 32, 256, 8, 4, 256], P(None, None, 'row', None, None, 'col')
Inputs may be any that keep to these rules, and one draw needn't show every extreme that they name: `target_rows`: each entry is a row of its front. Call the grid row of a front row i the value (i // 256) modulo the size of the row axis. Of the 256 rows of one row-axis index (an aligned block of one front), at most 16 have targets on any one grid row; in each front one grid row receives exactly 16 from every index.
All inputs are finite; a program needn't handle non-finite values.
Results may differ from a plain program's by a relative error of at most 0.00005.
Values sent between devices are 32-bit elements; how exact they have to be, the bound alone decides.
No kernel may reach another device: no remote copies, remote signals or barrier semaphores. Data moves between devices by JAX's collectives and lax.ppermute only.
A program may use at most 256 MiB of HBM per device.

v0:
```python
import jax
import jax.numpy as jnp
from jax import lax
from jax.experimental import pallas as pl
from jax.experimental.pallas import tpu as pltpu
from jax.sharding import PartitionSpec as P

F = 8192
P_SIZE = 1024
BS = 256
HI = lax.Precision.HIGHEST
LOW = 384
VM = pl.BlockSpec(memory_space=pltpu.VMEM)
SM = pl.BlockSpec(memory_space=pltpu.SMEM)
F32 = jnp.float32


def params():
    return pltpu.CompilerParams(vmem_limit_bytes=60 * 1024 * 1024)


def dot_nn(a, b):
    return lax.dot_general(a, b, (((1,), (0,)), ((), ())), precision=HI, preferred_element_type=F32)


def dot_nt(a, b):
    return lax.dot_general(a, b, (((1,), (1,)), ((), ())), precision=HI, preferred_element_type=F32)


def dot_tn(a, b):
    return lax.dot_general(a, b, (((0,), (0,)), ((), ())), precision=HI, preferred_element_type=F32)


def head_kernel(pos_ref, t_ref, x_ref, diag_ref, panel_ref, marks_ref, slots_ref, cnt):
    my_col = pos_ref[1]

    def clear(i, _):
        cnt[i] = 0
        for k in range(16):
            marks_ref[i // 2, (i % 2) * 16 + k] = 256
        return 0

    lax.fori_loop(0, 64, clear, 0)
    for i in range(32):
        panel_ref[pl.ds(i * 72 + 64, 2), :] = diag_ref[i // 16]

    def place_rows(group, _):
        first = pl.multiple_of(group * 8, 8)
        for f in range(2):
            for k in range(8):
                target = t_ref[f, first + k]
                owner = lax.shift_right_logical(target, 8)
                slot = cnt[f * 32 + owner]
                cnt[f * 32 + owner] = slot + 1
                marks_ref[owner, f * 16 + slot] = jnp.bitwise_and(target, 255)
                slots_ref[f, first + k] = owner * 128 + slot

                @pl.when(owner < 4)
                def _():
                    for j in range(16):
                        u, c, h = j // 8, (j // 2) % 4, j % 2
                        q = jnp.bitwise_and(c + 4 - my_col, 3)
                        dest = f * 16 + u * 8 + q * 2 + h
                        panel_ref[pl.ds(dest * 72 + owner * 16 + slot, 1), :] = (
                            x_ref[f, pl.ds(first, 8), j * 128:(j + 1) * 128][k:k + 1, :]
                        )

        return 0

    lax.fori_loop(0, 32, place_rows, 0)


def build_head(pos, targets, contrib, diag):
    return pl.pallas_call(
        head_kernel,
        out_shape=(
            jax.ShapeDtypeStruct((32 * 72, 128), F32),
            jax.ShapeDtypeStruct((32, 32), jnp.int32),
            jax.ShapeDtypeStruct((2, 256), jnp.int32),
        ),
        in_specs=[SM, SM, VM, VM],
        out_specs=(VM, SM, SM),
        scratch_shapes=[pltpu.SMEM((64,), jnp.int32)],
        compiler_params=params(),
    )(pos, targets, contrib, diag)


def main_kernel(slots_ref, x_ref, main_ref, buf):
    for f in range(2):
        for j in range(16):
            block, half = j // 2, j % 2
            place = (block % 4) * 4 + (block // 4) * 2 + half
            buf[pl.ds(f * 4096 + place, 256, stride=16), :] = x_ref[f, :, j * 128:(j + 1) * 128]

    def place_row(i, _):
        for f in range(2):
            at = slots_ref[f, i]
            source = (f * 256 + i) * 16
            for c in range(4):
                main_ref[pl.ds((at + (c * 2 + f) * 16) * 4, 4), :] = buf[pl.ds(source + c * 4, 4), :]
        return 0

    lax.fori_loop(0, 256, place_row, 0, unroll=2)


def build_main(slots, contrib):
    return pl.pallas_call(
        main_kernel,
        out_shape=jax.ShapeDtypeStruct((16384, 128), F32),
        in_specs=[SM, VM],
        out_specs=VM,
        scratch_shapes=[pltpu.VMEM((8192, 128), F32)],
        compiler_params=params(),
        cost_estimate=pl.CostEstimate(flops=10**10, bytes_accessed=2**23, transcendentals=0),
    )(slots, contrib)


def eye128():
    return (
        lax.broadcasted_iota(jnp.int32, (128, 128), 0) == lax.broadcasted_iota(jnp.int32, (128, 128), 1)
    ).astype(F32)


def panel_kernel(pos_ref, marks_ref, pattern_ref, x_ref, out_ref, acc):
    my_row, my_col = pos_ref[0], pos_ref[1]
    f, u, q, h = my_row // 16, (my_row // 8) % 2, (my_row // 2) % 4, my_row % 2
    block = 8 * my_col + u * 4 + (q + my_col) % 4
    acc[...] = jnp.zeros_like(acc)

    def source(s, _):
        def step(k, _):
            rows = [n * 264 + marks_ref[s, 32 + n * 16 + k] for n in range(4)]
            new = [
                acc[pl.ds(rows[n], 1), :] + x_ref[pl.ds(s * 72 + n * 16 + k, 1), :] for n in range(4)
            ]
            for n in range(4):
                acc[pl.ds(rows[n], 1), :] = new[n]
            return 0

        return lax.fori_loop(0, 16, step, 0, unroll=4)

    lax.fori_loop(0, 32, source, 0)
    scale = jnp.where(block >= 4, pattern_ref[f, block], 1).astype(F32)
    for n in range(4):
        out_ref[pl.ds(n * 256, 256), :] = acc[n * 264:n * 264 + 256, :] * scale

    @pl.when(block < 4)
    def _():
        start = pl.multiple_of(block * 256 + h * 128, 128)
        shift = x_ref[pl.ds(block * 72 + 64 + h, 1), :]
        out_ref[pl.ds(start, 128), :] += eye128() * shift


def panel_piece(pos, marks, pattern, received):
    return pl.pallas_call(
        panel_kernel,
        out_shape=jax.ShapeDtypeStruct((1024, 128), F32),
        in_specs=[SM, SM, SM, VM],
        out_specs=VM,
        scratch_shapes=[pltpu.VMEM((1056, 128), F32)],
        compiler_params=params(),
    )(pos, marks, pattern, received)


SRCS = 8


def assemble_kernel(pos_ref, marks_ref, pattern_ref, diag_ref, x_ref, out_ref, left_ref, acc):
    step = pl.program_id(0)
    my_row, my_col = pos_ref[0], pos_ref[1]

    @pl.when(step == 0)
    def _():
        acc[...] = jnp.zeros_like(acc)

    def source(s, _):
        def slot(k, _):
            at = [marks_ref[step * SRCS + s, f * 16 + k] * 16 for f in range(2)]
            new = [
                acc[f, pl.ds(at[f] + c * 4, 4), :]
                + x_ref[pl.ds((((s * 4 + c) * 2 + f) * 16 + k) * 4, 4), :]
                for f in range(2) for c in range(4)
            ]
            for f in range(2):
                for c in range(4):
                    acc[f, pl.ds(at[f] + c * 4, 4), :] = new[f * 4 + c]
            return 0

        return lax.fori_loop(0, 16, slot, 0)

    lax.fori_loop(0, SRCS, source, 0)

    @pl.when(step == pl.num_programs(0) - 1)
    def _():
        for f in range(2):
            scale = jnp.where(my_row >= 4, pattern_ref[f, my_row], 1).astype(F32)

            @pl.when(my_row % 4 == my_col)
            def _():
                for h in range(2):
                    at = pl.ds(h * 2048 + (my_row // 4) * 2 + h, 128, stride=16)
                    acc[f, at, :] += eye128() * diag_ref[f, h:h + 1, :]

            for h in range(2):
                left_ref[f, :, h * 128:(h + 1) * 128] = acc[f, pl.ds(h, 256, stride=16), :] * scale
            out_ref[f] = acc[f, :4096, :]


def assemble(pos, marks, pattern, diag, received):
    chunk = SRCS * 512
    return pl.pallas_call(
        assemble_kernel,
        grid=(32 // SRCS,),
        out_shape=(
            jax.ShapeDtypeStruct((2, 4096, 128), F32),
            jax.ShapeDtypeStruct((2, 256, 256), F32),
        ),
        in_specs=[SM, SM, SM, VM, pl.BlockSpec((chunk, 128), lambda s: (s, 0))],
        out_specs=(
            pl.BlockSpec((2, 4096, 128), lambda s: (0, 0, 0)),
            pl.BlockSpec((2, 256, 256), lambda s: (0, 0, 0)),
        ),
        scratch_shapes=[pltpu.VMEM((2, 4112, 128), F32)],
        compiler_params=params(),
        cost_estimate=pl.CostEstimate(flops=10**6, bytes_accessed=2**12, transcendentals=0),
    )(pos, marks, pattern, diag, received)


def factor_steps(steps, l_ref, x_ref, d_ref):
    lanes = lax.broadcasted_iota(jnp.int32, (8, 128), 1)
    subs = lax.broadcasted_iota(jnp.int32, (8, 128), 0)
    low = lax.broadcasted_iota(jnp.int32, (128, 128), 0) >= lax.broadcasted_iota(jnp.int32, (128, 128), 1)

    for p in steps:
        here = slice(p * 128, (p + 1) * 128)
        d_ref[:, :128] = l_ref[here, here]
        d_ref[:, 128:] = eye128()

        def group(g, _):
            rows = d_ref[pl.ds(pl.multiple_of(g * 8, 8), 8), :]
            a8, r8 = rows[:, :128], rows[:, 128:]
            turned = pltpu.roll(a8, (128 - g * 8) % 128, 1)
            cols = [jnp.broadcast_to(turned[:, j:j + 1], (8, 128)) for j in range(8)]
            for j in range(8):
                pivot = jnp.broadcast_to(cols[j][j:j + 1, :], (8, 128))
                root = lax.rsqrt(pivot)
                root = root * (1.5 - 0.5 * pivot * root * root)
                mult = jnp.where(subs > j, cols[j] * root, 0.0)
                for k in range(j + 1, 8):
                    cols[k] = cols[k] - mult * (cols[k][j:j + 1, :] * root)
                ua, ur = a8[j:j + 1, :] * root, r8[j:j + 1, :] * root
                a8 = jnp.where(subs == j, ua, a8 - mult * ua)
                r8 = jnp.where(subs == j, ur, r8 - mult * ur)
            new = jnp.concatenate([a8, r8], axis=1)
            d_ref[pl.ds(pl.multiple_of(g * 8, 8), 8), :] = new
            later = jnp.where(lanes > g * 8 + 7, a8, 0.0)
            d_ref[...] = d_ref[...] - dot_tn(later, new)
            return 0

        lax.fori_loop(0, 16, group, 0)
        inverse = jnp.where(low, d_ref[:, 128:], 0.0)
        l_ref[here, here] = jnp.where(low, d_ref[:, :128].T, 0.0)
        x_ref[here, here] = inverse
        if p > 0:
            done = p * 128
            both = dot_nn(l_ref[here, :done], x_ref[:done, :done])
            x_ref[here, :done] = -dot_nn(inverse, both)
        if p < 7:
            after = (p + 1) * 128
            l_ref[here, after:] = jnp.zeros((128, 1024 - after), F32)
            x_ref[here, after:] = jnp.zeros((128, 1024 - after), F32)
            l_ref[after:, here] = dot_nt(l_ref[after:, here], inverse)
            for i in range(p + 1, 8):
                mine = slice(i * 128, (i + 1) * 128)
                upto = slice(after, (i + 1) * 128)
                l_ref[mine, upto] = l_ref[mine, upto] - dot_nt(l_ref[mine, here], l_ref[upto, here])


def factor_kernel(pos_ref, lo_ref, hi_ref, l_ref, x_ref, d_ref):
    my_z = (pos_ref[0] // 2) % 4

    def corner(rows, block):
        ref, first = (lo_ref, rows * 128) if rows * 128 < LOW else (hi_ref, rows * 128 - LOW)
        return ref[jnp.bitwise_and(my_z + 4 - block // 2, 3), block % 2, first:first + 128, :]

    for i in range(8):
        for j in range(i + 1):
            l_ref[i * 128:(i + 1) * 128, j * 128:(j + 1) * 128] = 0.5 * (corner(i, j) + corner(j, i).T)
    factor_steps(range(8), l_ref, x_ref, d_ref)


def factor(pos, corner_lo, corner_hi):
    whole = jax.ShapeDtypeStruct((1024, 1024), F32)
    return pl.pallas_call(
        factor_kernel,
        out_shape=(whole, whole),
        in_specs=[SM, VM, VM],
        out_specs=(VM, VM),
        scratch_shapes=[pltpu.VMEM((128, 256), F32)],
        compiler_params=params(),
        cost_estimate=pl.CostEstimate(flops=10**11, bytes_accessed=12 * 2**20, transcendentals=0),
    )(pos, corner_lo, corner_hi)


def left_kernel(pos_ref, a_ref, x_ref, head_ref, w_ref, wide, rows):
    my_row, my_col = pos_ref[0], pos_ref[1]
    for far in range(2):
        for core in range(2):
            column = jnp.bitwise_xor(my_col, core + 2 * far)
            wide[:, pl.ds(pl.multiple_of(column * 256, 256), 256)] = a_ref[far, core]
    for b in range(4):
        here = slice(b * 256, (b + 1) * 256)
        rows[:, here] = dot_nt(wide[:, :(b + 1) * 256], x_ref[here, :(b + 1) * 256])
    for b in range(4):
        here = slice(b * 256, (b + 1) * 256)
        w_ref[:, here] = dot_nn(rows[:, b * 256:], x_ref[b * 256:, here])

    @pl.when(my_row < 4)
    def _():
        rows[...] = head_ref[...]

    for core in range(2):
        column = pl.multiple_of(jnp.bitwise_xor(my_col, core) * 256, 256)
        w_ref[:, 1024 + core * 256:1280 + core * 256] = rows[:, pl.ds(column, 256)]


def left(pos, a, inverse, lower):
    return pl.pallas_call(
        left_kernel,
        grid_spec=pltpu.PrefetchScalarGridSpec(
            num_scalar_prefetch=1,
            grid=(1,),
            in_specs=[
                pl.BlockSpec((2, 2, 256, 256), lambda i, pos: (0, 0, 0, 0)),
                pl.BlockSpec((1024, 1024), lambda i, pos: (0, 0)),
                pl.BlockSpec((256, 1024), lambda i, pos: (jnp.minimum(pos[0], 3), 0)),
            ],
            out_specs=pl.BlockSpec((256, 1536), lambda i, pos: (0, 0)),
            scratch_shapes=[pltpu.VMEM((256, 1024), F32), pltpu.VMEM((256, 1024), F32)],
        ),
        out_shape=jax.ShapeDtypeStruct((256, 1536), F32),
        compiler_params=params(),
        cost_estimate=pl.CostEstimate(flops=10**6, bytes_accessed=2**12, transcendentals=0),
    )(pos, a, inverse, lower)


def split(value):
    high = value.astype(jnp.bfloat16)
    return high, (value - high.astype(F32)).astype(jnp.bfloat16)


def dot_16(a, b):
    return lax.dot_general(a, b, (((1,), (0,)), ((), ())), preferred_element_type=F32)


def schur_kernel(table_ref, front_ref, w_ref, *refs):
    out_ref, partial, w_high, w_low = refs[10:]
    f, j = pl.program_id(0), pl.program_id(1)
    my_row = table_ref[144]
    par = jnp.bitwise_and(my_row, 1)
    block = 2 * jnp.bitwise_and(j, 3) + lax.shift_right_logical(j, 2)
    turned = (table_ref[f * 8 + j], table_ref[16 + f * 8 + j])
    places = [pl.ds(2 * block + h, 256, stride=16) for h in range(2)]

    def columns(ref, rows):
        return jnp.concatenate([ref[0, jnp.bitwise_xor(par, h), rows, :] for h in range(2)], axis=1)

    def put(value):
        for h in range(2):
            out_ref[0, places[h], :] = value[:, h * 128:(h + 1) * 128]

    @pl.when(j == 0)
    def _():
        put(w_ref[0, :, 1024:1280])
        w_high[...], w_low[...] = split(w_ref[0, :, :1024])

    for part in range(2):
        own, below, first, second, above = refs[5 * part:5 * part + 5]
        for k, sources in enumerate(((own,), (below,), (first, second), (above,))):
            here = (j > 0) & (turned[part] == k)
            rows = 512 // len(sources)

            @pl.when(here & (my_row >= 4))
            def _():
                total = 0.0
                for i, ref in enumerate(sources):
                    start = part * 512 + i * rows
                    high, low = split(columns(ref, slice(0, rows)))
                    own_high, own_low = w_high[:, start:start + rows], w_low[:, start:start + rows]
                    total += dot_16(own_high, low) + dot_16(own_low, high) + dot_16(own_high, high)
                if part == 0:
                    partial[...] = total
                else:
                    total = total + partial[...]
                    for h in range(2):
                        out_ref[0, places[h], :] = (
                            front_ref[0, places[h], :] - total[:, h * 128:(h + 1) * 128]
                        )

            for i in range(2):

                @pl.when(here & (my_row == part * 2 + i))
                def _():
                    if len(sources) == 2:
                        put(columns(sources[i], slice(0, 256)))
                    else:
                        put(columns(sources[0], slice(i * 256, (i + 1) * 256)))


def schur_steps(pos):
    step = jnp.arange(16, dtype=jnp.int32)
    x, z = step // 4, (pos[1] + 4 - step % 4) % 4
    my_x, my_z = pos[0] // 8, (pos[0] // 2) % 4
    rows = [(my_x + 4 - x) % 4, (my_z + 4 - z) % 4]
    for k in (0, 1, 2, 2, 3):
        mine = (my_x + 4 - k) % 4
        idle = jnp.where(x < mine, z[0], z[3])
        rows.append(jnp.where(x == mine, z, idle))
    rows.append(x)
    rows.append(jnp.broadcast_to(pos[1] % 2, (16,)))
    return jnp.concatenate([jnp.concatenate(rows), pos]).astype(jnp.int32)


def schur(pos, front, w, lo, hi):
    def lo_map(row):
        return lambda f, j, table: (table[row * 16 + f * 8 + j], 0, 0, 0)

    def fixed(f, j, table):
        return f, 0, 0

    rows = (512, 512, 256, 256, 512)
    return pl.pallas_call(
        schur_kernel,
        grid_spec=pltpu.PrefetchScalarGridSpec(
            num_scalar_prefetch=1,
            grid=(2, 8),
            in_specs=[
                pl.BlockSpec((1, 4096, 128), fixed),
                pl.BlockSpec(
                    (1, 256, 1280), lambda f, j, table: (jnp.bitwise_xor(f, table[128]), 0, 0)
                ),
            ]
            + [pl.BlockSpec((1, 2, n, 128), lo_map(2 + i)) for i, n in enumerate(rows)]
            + [pl.BlockSpec((1, 2, n, 128), lo_map(7)) for n in rows],
            out_specs=pl.BlockSpec((1, 4096, 128), fixed),
            scratch_shapes=[
                pltpu.VMEM((256, 256), F32),
                pltpu.VMEM((256, 1024), jnp.bfloat16),
                pltpu.VMEM((256, 1024), jnp.bfloat16),
            ],
        ),
        out_shape=jax.ShapeDtypeStruct((2, 4096, 128), F32),
        compiler_params=params(),
    )(schur_steps(pos), front, w, *lo, *hi)


def turn(axis, by):
    pairs = []
    for x in range(4):
        for z in range(4):
            for y in range(2):
                to = ((x + by) % 4, z) if axis == "x" else (x, (z + by) % 4)
                pairs.append((x * 8 + z * 2 + y, to[0] * 8 + to[1] * 2 + y))
    return pairs


def ring(value, axis):
    forth, back = turn(axis, 1), turn(axis, -1)
    half = value.shape[-2] // 2
    below = lax.ppermute(value, "row", forth)
    above = lax.ppermute(value, "row", back)
    first = lax.ppermute(below[..., :half, :], "row", forth)
    second = lax.ppermute(above[..., half:, :], "row", back)
    return value, below, first, second, above


def gathered(value, axis):
    if axis == "x":
        groups = [[x * 8 + rest for x in range(4)] for rest in range(8)]
    else:
        groups = [[x * 8 + z * 2 + y for z in range(4)] for x in range(4) for y in range(2)]
    return lax.all_gather(value, "row", axis_index_groups=groups)


def across(value, pairs, axis):
    return jnp.stack([value, lax.ppermute(value, axis, pairs)])


CORE = [(0, 1), (1, 0), (2, 3), (3, 2)]
FAR = [(0, 2), (2, 0), (1, 3), (3, 1)]
NEAR = [(i, i ^ 1) for i in range(32)]


def own_front(value, my_core):
    kept = lax.dynamic_index_in_dim(value, my_core, 0, keepdims=False)
    given = lax.dynamic_index_in_dim(value, 1 - my_core, 0, keepdims=False)
    return across(jnp.stack([kept, lax.ppermute(given, "col", CORE)]), FAR, "col")


def device(x, z, y, core):
    return (x * 8 + z * 2 + y % 2) * 4 + (y // 2) * 2 + core


def corner_columns(piece, moved, my_x, my_z, my_y, my_core):
    both = ("row", "col")
    got = []
    for k in range(4):
        pairs = [
            (device(2 * f, z, h, 0), device(2 * f, z, (h + k) % 4, f))
            for f in range(2) for z in range(4) for h in range(2)
        ]
        got.append(lax.ppermute(piece, both, pairs))
    got, moved = lax.optimization_barrier((got, moved))
    got = jnp.stack(got)
    pair = jnp.stack(
        [lax.dynamic_index_in_dim(got, (my_y + 4 - h) % 4, 0, keepdims=False) for h in range(2)]
    )
    away = (my_x + 4 - 2 * my_core) % 4

    def spread_x(value):
        half = value.shape[-2] // 2

        def moved(part, start, by):
            pairs = [
                (device((2 * core + start) % 4, z, y, core), device((2 * core + start + by) % 4, z, y, core))
                for z in range(4) for y in range(4) for core in range(2)
            ]
            return lax.ppermute(part, both, pairs)

        below, above = moved(value, 0, 1), moved(value, 0, -1)
        if value.ndim == 3:
            far = moved(value, 0, 2)
        else:
            far = jnp.concatenate(
                [moved(below[..., :half, :], 1, 1), moved(above[..., half:, :], 3, -1)], axis=-2
            )
        return jnp.where(away == 0, value, jnp.where(away == 1, below, jnp.where(away == 3, above, far)))

    def ring_z(value, xs):
        def moved(part, by):
            pairs = [
                (device(x, z, y, core), device(x, (z + by) % 4, y, core))
                for z in range(4) for y in range(4) for core in range(2) for x in xs(core)
            ]
            return lax.ppermute(part, both, pairs)

        return jnp.stack([value] + [moved(value, by) for by in (1, 2, -1)])

    lo = ring_z(pair[:, :LOW], lambda core: [2 * core])
    hi = spread_x(pair[:, LOW:])
    near = across(moved, NEAR, "row")
    lo, hi, near = lax.optimization_barrier((lo, hi, near))
    return spread_x(lo), ring_z(hi, lambda core: range(4)), near


def shards(contrib, target_rows, diag_shift, pattern):
    my_row = lax.axis_index("row").astype(jnp.int32)
    my_col = lax.axis_index("col").astype(jnp.int32)
    my_core = my_col % 2
    my_x, my_z, my_y = my_row // 8, (my_row // 2) % 4, (my_col // 2) * 2 + my_row % 2
    pos = jnp.stack([my_row, my_col])
    diag = diag_shift.reshape(2, 2, 128)
    panel, marks, slots = build_head(pos, target_rows, contrib, diag)
    heads = jnp.swapaxes(marks[:4].reshape(4, 2, 16), 0, 1).reshape(2, 1, 64)
    heads = jnp.broadcast_to(heads, (2, 16, 64)).reshape(32, 64)
    marks = jnp.concatenate([marks, heads, heads[:, :32]], axis=1).astype(F32)
    panel = panel.reshape(32, 72, 128).at[:, 66, :].set(marks)
    panel = lax.all_to_all(panel, "row", split_axis=0, concat_axis=0, tiled=True)
    marks = panel[:, 66, :96].astype(jnp.int32)
    piece = panel_piece(pos, marks, pattern, panel.reshape(32 * 72, 128))
    slots, piece = lax.optimization_barrier((slots, piece))
    main = build_main(slots, contrib)
    moves = [
        (i * 4 + c, i * 4 + ((i // 2) % 4 + c) % 4) for i in range(32) for c in range(4)
    ]
    moved = lax.ppermute(piece, ("row", "col"), moves)
    corner_lo, corner_hi, pair = corner_columns(piece, moved, my_x, my_z, my_y, my_core)
    corner_lo, corner_hi, main, pair = lax.optimization_barrier((corner_lo, corner_hi, main, pair))
    lo, hi = gathered(pair[:, :512], "z"), gathered(pair[:, 512:], "x")
    main = lax.all_to_all(
        main.reshape(128, 128, 128), ("row", "col"), split_axis=0, concat_axis=0, tiled=True
    )
    lower, inverse = factor(pos, corner_lo, corner_hi)
    main, lower, lo, hi = lax.optimization_barrier((main, lower, lo, hi))
    lo, hi = ring(lo, "x"), ring(hi, "z")
    front, own_left = assemble(pos, marks, pattern, diag, main.reshape(16384, 128))
    lefts = own_front(own_left, my_core)
    w = left(pos, lefts, inverse, lower)
    kept = w[:, :1280]
    given = jnp.concatenate([w[:, :1024], w[:, 1280:]], axis=1)
    w = jnp.stack([kept, lax.ppermute(given, "col", CORE)])
    result = schur(pos, front, w, lo, hi)
    return result.reshape(2, 1, 1, 256, 8, 1, 256)


def solution(mesh):
    in_specs = (P(None, "row", "col"), P(None, "row"), P(None, None, "row", None), P())
    out_specs = P(None, None, "row", None, None, "col", None)
    return jax.shard_map(shards, mesh=mesh, in_specs=in_specs, out_specs=out_specs, check_vma=False)
```

profile of v0, /device:TPU:6, one launch (start us, length us, event | category | flops | bytes accessed | tf_op | source)
XLA Modules:
  0.0 424.7 jit_solution(5223090869765317194)
XLA Ops:
  7.1 14.3 %shard_map.46 = (f32[2304,128]{1,0:T(8,128)}, s32[32,32]{1,0:T(8,128)}, s32[2,256]{1,0:T(2,128)}) custom-call(s32[2]{0:T(128)} %pad_add_fusion.pos_ref, s32[2,256]{1,0:T(2,128)} %t_ref.1, f32[2,256,2048]{2,1,0:T(8,128)} %x_ref.3, f32[2,2,128]{2,1,0:T(2,128)} %bitcast.71), custom_call_target="tpu_custom_call" | custom-call | tf_op jit(solution)/shard_map/pallas_call | solution.py:74
  23.2 1.6 scatter.4
  24.8 26.6 %all_to_all.10 = f32[32,72,128]{2,1,0:T(8,128)S(1)} all-to-all(f32[32,72,128]{2,1,0:T(8,128)} %scatter.4), channel_id=1, replica_groups=mesh['row'=32,'col'=4] {'row'}, dimensions={0} | all-to-all | bytes 2359296 | tf_op jit(solution)/shard_map/all_to_all | solution.py:568
  52.4 7.6 %shard_map.47 = f32[1024,128]{1,0:T(8,128)} custom-call(s32[2]{0:T(128)} %pad_add_fusion.pos_ref, s32[32,96]{1,0:T(8,128)} %convert_bitcast_fusion.marks_ref, s32[2,32]{1,0:T(2,128)} %pattern_ref.3, f32[2304,128]{1,0:T(8,128)} %bitcast.48), custom_call_target="tpu_custom_call" | custom-call | tf_op jit(solution)/shard_map/pallas_call | solution.py:155
  59.9 5.3 %collective-permute-start.4 = (f32[1024,128]{1,0:T(8,128)}, f32[1024,128]{1,0:T(8,128)}, u32[]{:S(2)}, u32[]{:S(2)}) collective-permute-start(f32[1024,128]{1,0:T(8,128)} %shard_map.47), channel_id=1, source_target_pairs={{0,0},{1,1},{2,2},{3,3},{4,4},{5,5},{6,6},{7,7},{8,9},{9,10},{10,1... | collective-permute-start | bytes 1572872 | tf_op jit(solution)/shard_map/ppermute | solution.py:576
  78.0 5.9 %collective-permute-done.11 = f32[1024,128]{1,0:T(8,128)} collective-permute-done((f32[1024,128]{1,0:T(8,128)}, f32[1024,128]{1,0:T(8,128)}, u32[]{:S(2)}, u32[]{:S(2)}) %collective-permute-start.11) | collective-permute-done | bytes 524320 | tf_op jit(solution)/shard_map/ppermute | solution.py:486
  83.9 2.3 pad_maximum_fusion.5
  86.2 30.8 %collective-permute-done.9 = f32[2,640,128]{2,1,0:T(8,128)} collective-permute-done((f32[2,640,128]{2,1,0:T(8,128)S(1)}, f32[2,640,128]{2,1,0:T(8,128)}, u32[]{:S(2)}, u32[]{:S(2)}) %collective-permute-start.9) | collective-permute-done | bytes 655392 | tf_op jit(solution)/shard_map/ppermute | solution.py:528
  122.4 24.1 %collective-permute-done.13 = f32[4,2,384,128]{3,2,1,0:T(8,128)S(1)} collective-permute-done((f32[4,2,384,128]{3,2,1,0:T(8,128)S(1)}, f32[4,2,384,128]{3,2,1,0:T(8,128)S(1)}, u32[]{:S(2)}, u32[]{:S(2)}) %collective-permute-start.13) | collective-permute-done | bytes 1572896 | tf_op jit(solution)/shard_map/ppermute | solution.py:528
  147.4 2.2 collective-permute-start.15
  151.7 1.5 collective-permute-start.14
  153.2 9.5 %shard_map.48 = f32[16384,128]{1,0:T(8,128)} custom-call(s32[2,256]{1,0:T(2,128)} %get-tuple-element.53.slots_ref, f32[2,256,2048]{2,1,0:T(8,128)} %x_ref.3), custom_call_target="tpu_custom_call" | custom-call | flops 10000000000 | bytes 8388608 | tf_op jit(solution)/shard_map/pallas_call | solution.py:107
  162.8 3.3 pad_maximum_fusion.hi_ref
  166.2 2.9 fusion.1.lo_ref
  170.1 6.0 %all-to-all-start.1 = ((f32[128,128,128]{2,1,0:T(8,128)}), f32[128,128,128]{2,1,0:T(8,128)}, u32[]{:S(2)}, u32[]{:S(2)}) async-start(f32[128,128,128]{2,1,0:T(8,128)} %bitcast.47), calls=%async_computation.1 | async-start | bytes 16777216 | tf_op jit(solution)/shard_map/all_to_all | solution.py:580
  176.9 100.7 %shard_map.49 = (f32[1024,1024]{1,0:T(8,128)}, f32[1024,1024]{1,0:T(8,128)}) custom-call(s32[2]{0:T(128)} %pad_add_fusion.pos_ref, f32[4,2,384,128]{3,2,1,0:T(8,128)} %fusion.1.lo_ref, f32[4,2,640,128]{3,2,1,0:T(8,128)} %pad_maximum_fusion.hi_ref), custom_call_target="tpu_custom_call" | custom-call | flops 99999997952 | bytes 12582912 | tf_op jit(solution)/shard_map/pallas_call | solution.py:294
  277.6 23.2 %all-gather.5.cloned.1.call-done = f32[8,512,128]{2,1,0:T(8,128)} async-done(((f32[2,512,128]{2,1,0:T(8,128)}), f32[8,512,128]{2,1,0:T(8,128)}) %all-gather.5.cloned.1.call-update) | async-done | bytes 2097168 | tf_op jit(solution)/shard_map/all_gather | solution.py:482
  301.9 2.1 collective-permute-start.22
  306.1 12.0 %shard_map.50 = (f32[2,4096,128]{2,1,0:T(8,128)}, f32[2,256,256]{2,1,0:T(8,128)}) custom-call(s32[2]{0:T(128)} %pad_add_fusion.pos_ref, s32[32,96]{1,0:T(8,128)} %convert_bitcast_fusion.marks_ref, s32[2,32]{1,0:T(2,128)} %pattern_ref.3, f32[2,2,128]{2,1,0:T(2,128)} %bitcast.72, f32[16384,128]{1,0:T(8,128)} %bitcast.31.x_ref), custom_call_target="tpu_custom_call" | custom-call | flops 1000000 | bytes 4096 | tf_op jit(solution)/shard_map/pallas_call | solution.py:211
  320.8 2.3 collective-permute-start.20
  323.1 13.5 %collective-permute-done.20 = f32[2,256,256]{2,1,0:T(8,128)S(1)} collective-permute-done((f32[2,256,256]{2,1,0:T(8,128)S(1)}, f32[2,256,256]{2,1,0:T(8,128)S(1)}, u32[]{:S(2)}, u32[]{:S(2)}) %collective-permute-start.20) | collective-permute-done | bytes 524320 | tf_op jit(solution)/shard_map/ppermute | solution.py:486
  337.6 9.6 %shard_map.51 = f32[256,1536]{1,0:T(8,128)} custom-call(s32[2]{0:T(128)} %pad_add_fusion.pos_ref, f32[2,2,256,256]{3,2,1,0:T(8,128)} %pad_maximum_fusion.6.a_ref, f32[1024,1024]{1,0:T(8,128)} %get-tuple-element.63.x_ref, f32[1024,1024]{1,0:T(8,128)} %get-tuple-element.64.head_ref), custom_call_target="tpu_custom_call" | custom-call | flops 1000000 | bytes 4096 | tf_op jit(solution)/shard_map/pallas_call | solution.py:328
  353.1 2.3 slice.107
  355.4 2.8 collective-permute-start.23
  358.2 2.3 slice.110
  360.5 2.6 collective-permute-start.29
  363.1 2.3 slice.109
  367.4 3.1 pad_maximum_fusion.1.w_ref
  370.6 9.3 %collective-permute-done.25.refs_3_ = f32[4,2,256,128]{3,2,1,0:T(8,128)} collective-permute-done((f32[4,2,256,128]{3,2,1,0:T(8,128)}, f32[4,2,256,128]{3,2,1,0:T(8,128)}, u32[]{:S(2)}, u32[]{:S(2)}) %collective-permute-start.25) | collective-permute-done | bytes 1048608 | tf_op jit(solution)/shard_map/ppermute | solution.py:473
  381.4 4.6 %collective-permute-done.29.refs_8_ = f32[4,2,256,128]{3,2,1,0:T(8,128)} collective-permute-done((f32[4,2,256,128]{3,2,1,0:T(8,128)}, f32[4,2,256,128]{3,2,1,0:T(8,128)}, u32[]{:S(2)}, u32[]{:S(2)}) %collective-permute-start.29) | collective-permute-done | bytes 1048608 | tf_op jit(solution)/shard_map/ppermute | solution.py:473
  386.0 5.7 %collective-permute-done.27.refs_7_ = f32[4,2,256,128]{3,2,1,0:T(8,128)} collective-permute-done((f32[4,2,256,128]{3,2,1,0:T(8,128)}, f32[4,2,256,128]{3,2,1,0:T(8,128)}, u32[]{:S(2)}, u32[]{:S(2)}) %collective-permute-start.27) | collective-permute-done | bytes 1048608 | tf_op jit(solution)/shard_map/ppermute | solution.py:472
  391.6 25.8 %shard_map.52 = f32[2,4096,128]{2,1,0:T(8,128)} custom-call(s32[146]{0:T(256)} %concatenate.26.table_ref, f32[2,4096,128]{2,1,0:T(8,128)} %get-tuple-element.61.front_ref, f32[2,256,1280]{2,1,0:T(8,128)} %pad_maximum_fusion.1.w_ref, f32[4,2,512,128]{3,2,1,0:T(8,128)} %bitcast.55, f32[4,2,512,128]{3,2,1,0:T(8,128)} %collective-permute-done.22.refs_1_, ...), custom_call_target="tpu_custom_call" | custom-call | tf_op jit(solution)/shard_map/pallas_call | solution.py:432
  (109 shorter events, 42.5 us)
Async XLA Ops:
  6.5 271.1 %all-gather.7.cloned.1.call-start = ((), (), s32[]{:S(2)}) async-start(), calls=%async_computation.3 | async-start | bytes 2621440 | tf_op jit(solution)/shard_map/all_gather | solution.py:482
  59.9 8.2 %collective-permute-start.4 = (f32[1024,128]{1,0:T(8,128)}, f32[1024,128]{1,0:T(8,128)}, u32[]{:S(2)}, u32[]{:S(2)}) collective-permute-start(f32[1024,128]{1,0:T(8,128)} %shard_map.47), channel_id=1, source_target_pairs={{0,0},{1,1},{2,2},{3,3},{4,4},{5,5},{6,6},{7,7},{8,9},{9,10},{10,1... | collective-permute-start | bytes 1572872 | tf_op jit(solution)/shard_map/ppermute | solution.py:576
  65.3 2.9 collective-permute-start.3
  65.9 2.2 collective-permute-start.2
  66.6 1.5 collective-permute-start.1
  68.4 4.4 %collective-permute-start.6 = (f32[2,384,128]{2,1,0:T(8,128)S(1)}, f32[2,384,128]{2,1,0:T(8,128)S(1)}, u32[]{:S(2)}, u32[]{:S(2)}) collective-permute-start(f32[2,384,128]{2,1,0:T(8,128)S(1)} %pad_maximum_fusion.9), channel_id=1, source_target_pairs={{0,16},{65,81},{4,20},{69,85},{2,18},{67,83},{6,22},{71,87},{8,24}... | collective-permute-start | bytes 1179656 | tf_op jit(solution)/shard_map/ppermute | solution.py:545
  69.1 5.3 %collective-permute-start.5 = (f32[2,384,128]{2,1,0:T(8,128)S(1)}, f32[2,384,128]{2,1,0:T(8,128)S(1)}, u32[]{:S(2)}, u32[]{:S(2)}) collective-permute-start(f32[2,384,128]{2,1,0:T(8,128)S(1)} %pad_maximum_fusion.9), channel_id=1, source_target_pairs={{0,8},{65,73},{4,12},{69,77},{2,10},{67,75},{6,14},{71,79},{8,16},... | collective-permute-start | bytes 1179656 | tf_op jit(solution)/shard_map/ppermute | solution.py:545
  69.8 6.1 %collective-permute-start.7 = (f32[2,384,128]{2,1,0:T(8,128)S(1)}, f32[2,384,128]{2,1,0:T(8,128)S(1)}, u32[]{:S(2)}, u32[]{:S(2)}) collective-permute-start(f32[2,384,128]{2,1,0:T(8,128)S(1)} %pad_maximum_fusion.9), channel_id=1, source_target_pairs={{0,24},{65,89},{4,28},{69,93},{2,26},{67,91},{6,30},{71,95},{8,0},... | collective-permute-start | bytes 1179656 | tf_op jit(solution)/shard_map/ppermute | solution.py:545
  70.5 13.4 %collective-permute-start.11 = (f32[1024,128]{1,0:T(8,128)}, f32[1024,128]{1,0:T(8,128)}, u32[]{:S(2)}, u32[]{:S(2)}) collective-permute-start(f32[1024,128]{1,0:T(8,128)} %collective-permute-done.4), channel_id=1, source_target_pairs={{0,4},{4,0},{8,12},{12,8},{16,20},{20,16},{24,28},{28,24},{32,36},... | collective-permute-start | bytes 1572872 | tf_op jit(solution)/shard_map/ppermute | solution.py:486
  71.6 45.4 %collective-permute-start.9 = (f32[2,640,128]{2,1,0:T(8,128)S(1)}, f32[2,640,128]{2,1,0:T(8,128)}, u32[]{:S(2)}, u32[]{:S(2)}) collective-permute-start(f32[2,640,128]{2,1,0:T(8,128)S(1)} %pad_maximum_fusion.7), channel_id=1, source_target_pairs={{0,96},{65,33},{4,100},{69,37},{2,98},{67,35},{6,102},{71,39},{8,1... | collective-permute-start | bytes 1966088 | tf_op jit(solution)/shard_map/ppermute | solution.py:528
  72.9 44.1 %collective-permute-start.8 = (f32[2,640,128]{2,1,0:T(8,128)S(1)}, f32[2,640,128]{2,1,0:T(8,128)}, u32[]{:S(2)}, u32[]{:S(2)}) collective-permute-start(f32[2,640,128]{2,1,0:T(8,128)S(1)} %pad_maximum_fusion.7), channel_id=1, source_target_pairs={{0,32},{65,97},{4,36},{69,101},{2,34},{67,99},{6,38},{71,103},{8,4... | collective-permute-start | bytes 1966088 | tf_op jit(solution)/shard_map/ppermute | solution.py:528
  74.4 42.6 %collective-permute-start.10 = (f32[2,640,128]{2,1,0:T(8,128)S(1)}, f32[2,640,128]{2,1,0:T(8,128)}, u32[]{:S(2)}, u32[]{:S(2)}) collective-permute-start(f32[2,640,128]{2,1,0:T(8,128)S(1)} %pad_maximum_fusion.7), channel_id=1, source_target_pairs={{0,64},{65,1},{4,68},{69,5},{2,66},{67,3},{6,70},{71,7},{8,72},{73... | collective-permute-start | bytes 1966088 | tf_op jit(solution)/shard_map/ppermute | solution.py:528
  118.2 28.3 %collective-permute-start.13 = (f32[4,2,384,128]{3,2,1,0:T(8,128)S(1)}, f32[4,2,384,128]{3,2,1,0:T(8,128)S(1)}, u32[]{:S(2)}, u32[]{:S(2)}) collective-permute-start(f32[4,2,384,128]{3,2,1,0:T(8,128)S(1)} %pad_maximum_fusion.3), channel_id=1, source_target_pairs={{0,96},{65,33},{4,100},{69,37},{2,98},{67,35},{6,102},{71,39},{8,1... | collective-permute-start | bytes 4718600 | tf_op jit(solution)/shard_map/ppermute | solution.py:528
  119.5 30.1 %collective-permute-start.12 = (f32[4,2,384,128]{3,2,1,0:T(8,128)S(1)}, f32[4,2,384,128]{3,2,1,0:T(8,128)S(1)}, u32[]{:S(2)}, u32[]{:S(2)}) collective-permute-start(f32[4,2,384,128]{3,2,1,0:T(8,128)S(1)} %pad_maximum_fusion.3), channel_id=1, source_target_pairs={{0,32},{65,97},{4,36},{69,101},{2,34},{67,99},{6,38},{71,103},{8,4... | collective-permute-start | bytes 4718600 | tf_op jit(solution)/shard_map/ppermute | solution.py:528
  120.3 42.5 %collective-permute-start.18 = (f32[2,640,128]{2,1,0:T(8,128)S(1)}, f32[2,640,128]{2,1,0:T(8,128)}, u32[]{:S(2)}, u32[]{:S(2)}) collective-permute-start(f32[2,640,128]{2,1,0:T(8,128)S(1)} %select_select_fusion), channel_id=1, source_target_pairs={{0,24},{32,56},{64,88},{96,120},{1,25},{33,57},{65,89},{97,121},{4... | collective-permute-start | bytes 1966088 | tf_op jit(solution)/shard_map/ppermute | solution.py:545
  120.4 42.4 %collective-permute-start.17 = (f32[2,640,128]{2,1,0:T(8,128)S(1)}, f32[2,640,128]{2,1,0:T(8,128)}, u32[]{:S(2)}, u32[]{:S(2)}) collective-permute-start(f32[2,640,128]{2,1,0:T(8,128)S(1)} %select_select_fusion), channel_id=1, source_target_pairs={{0,16},{32,48},{64,80},{96,112},{1,17},{33,49},{65,81},{97,113},{4... | collective-permute-start | bytes 1966088 | tf_op jit(solution)/shard_map/ppermute | solution.py:545
  121.2 41.6 %collective-permute-start.16 = (f32[2,640,128]{2,1,0:T(8,128)S(1)}, f32[2,640,128]{2,1,0:T(8,128)}, u32[]{:S(2)}, u32[]{:S(2)}) collective-permute-start(f32[2,640,128]{2,1,0:T(8,128)S(1)} %select_select_fusion), channel_id=1, source_target_pairs={{0,8},{32,40},{64,72},{96,104},{1,9},{33,41},{65,73},{97,105},{4,1... | collective-permute-start | bytes 1966088 | tf_op jit(solution)/shard_map/ppermute | solution.py:545
  147.4 18.8 %collective-permute-start.15 = (f32[4,2,192,128]{3,2,1,0:T(8,128)}, f32[4,2,192,128]{3,2,1,0:T(8,128)}, u32[]{:S(2)}, u32[]{:S(2)}) collective-permute-start(f32[4,2,192,128]{3,2,1,0:T(8,128)} %slice.103), channel_id=1, source_target_pairs={{96,64},{33,1},{100,68},{37,5},{98,66},{35,3},{102,70},{39,7},{104... | collective-permute-start | bytes 2359304 | tf_op jit(solution)/shard_map/ppermute | solution.py:528
  151.7 14.4 %collective-permute-start.14 = (f32[4,2,192,128]{3,2,1,0:T(8,128)}, f32[4,2,192,128]{3,2,1,0:T(8,128)}, u32[]{:S(2)}, u32[]{:S(2)}) collective-permute-start(f32[4,2,192,128]{3,2,1,0:T(8,128)} %slice.102), channel_id=1, source_target_pairs={{32,64},{97,1},{36,68},{101,5},{34,66},{99,3},{38,70},{103,7},{40,... | collective-permute-start | bytes 2359304 | tf_op jit(solution)/shard_map/ppermute | solution.py:528
  170.1 130.7 %all-to-all-start.1 = ((f32[128,128,128]{2,1,0:T(8,128)}), f32[128,128,128]{2,1,0:T(8,128)}, u32[]{:S(2)}, u32[]{:S(2)}) async-start(f32[128,128,128]{2,1,0:T(8,128)} %bitcast.47), calls=%async_computation.1 | async-start | bytes 16777216 | tf_op jit(solution)/shard_map/all_to_all | solution.py:580
  176.1 124.7 %all-gather.5.cloned.1.call-start = ((), (), s32[]{:S(2)}) async-start(), calls=%async_computation.2 | async-start | bytes 2621440 | tf_op jit(solution)/shard_map/all_gather | solution.py:482
  300.8 50.7 %collective-permute-start.24 = (f32[4,2,512,128]{3,2,1,0:T(8,128)}, f32[4,2,512,128]{3,2,1,0:T(8,128)S(1)}, u32[]{:S(2)}, u32[]{:S(2)}) collective-permute-start(f32[4,2,512,128]{3,2,1,0:T(8,128)} %bitcast.53), channel_id=1, source_target_pairs={{0,96},{4,100},{8,104},{12,108},{16,112},{20,116},{24,120},{28,124... | collective-permute-start | bytes 6291464 | tf_op jit(solution)/shard_map/ppermute | solution.py:471
  301.9 50.8 %collective-permute-start.22 = (f32[4,2,512,128]{3,2,1,0:T(8,128)}, f32[4,2,512,128]{3,2,1,0:T(8,128)}, u32[]{:S(2)}, u32[]{:S(2)}) collective-permute-start(f32[4,2,512,128]{3,2,1,0:T(8,128)} %bitcast.54), channel_id=1, source_target_pairs={{0,32},{4,36},{8,40},{12,44},{16,48},{20,52},{24,56},{28,60},{32,6... | collective-permute-start | bytes 6291464 | tf_op jit(solution)/shard_map/ppermute | solution.py:470
  304.0 54.2 %collective-permute-start.28 = (f32[4,2,512,128]{3,2,1,0:T(8,128)}, f32[4,2,512,128]{3,2,1,0:T(8,128)}, u32[]{:S(2)}, u32[]{:S(2)}) collective-permute-start(f32[4,2,512,128]{3,2,1,0:T(8,128)} %bitcast.50), channel_id=1, source_target_pairs={{0,24},{4,28},{8,0},{12,4},{16,8},{20,12},{24,16},{28,20},{32,56},... | collective-permute-start | bytes 6291464 | tf_op jit(solution)/shard_map/ppermute | solution.py:471
  305.6 57.5 %collective-permute-start.26 = (f32[4,2,512,128]{3,2,1,0:T(8,128)}, f32[4,2,512,128]{3,2,1,0:T(8,128)}, u32[]{:S(2)}, u32[]{:S(2)}) collective-permute-start(f32[4,2,512,128]{3,2,1,0:T(8,128)} %bitcast.51), channel_id=1, source_target_pairs={{0,8},{4,12},{8,16},{12,20},{16,24},{20,28},{24,0},{28,4},{32,40},... | collective-permute-start | bytes 6291464 | tf_op jit(solution)/shard_map/ppermute | solution.py:470
  319.1 1.6 collective-permute-start.19
  320.8 15.8 %collective-permute-start.20 = (f32[2,256,256]{2,1,0:T(8,128)S(1)}, f32[2,256,256]{2,1,0:T(8,128)S(1)}, u32[]{:S(2)}, u32[]{:S(2)}) collective-permute-start(f32[2,256,256]{2,1,0:T(8,128)S(1)} %get-tuple-element.72), channel_id=1, source_target_pairs={{0,2},{2,0},{1,3},{3,1},{4,6},{6,4},{5,7},{7,5},{8,10},{10,8},{9,1... | collective-permute-start | bytes 1572872 | tf_op jit(solution)/shard_map/ppermute | solution.py:486
  349.7 17.7 %collective-permute-start.21 = (f32[256,1280]{1,0:T(8,128)}, f32[256,1280]{1,0:T(8,128)}, u32[]{:S(2)}, u32[]{:S(2)}) collective-permute-start(f32[256,1280]{1,0:T(8,128)} %pad_maximum_fusion.4), channel_id=1, source_target_pairs={{0,1},{1,0},{2,3},{3,2},{4,5},{5,4},{6,7},{7,6},{8,9},{9,8},{10,11... | collective-permute-start | bytes 3932168 | tf_op jit(solution)/shard_map/ppermute | solution.py:591
  352.7 27.1 %collective-permute-start.25 = (f32[4,2,256,128]{3,2,1,0:T(8,128)}, f32[4,2,256,128]{3,2,1,0:T(8,128)}, u32[]{:S(2)}, u32[]{:S(2)}) collective-permute-start(f32[4,2,256,128]{3,2,1,0:T(8,128)} %slice.108), channel_id=1, source_target_pairs={{0,96},{4,100},{8,104},{12,108},{16,112},{20,116},{24,120},{28,124... | collective-permute-start | bytes 3145736 | tf_op jit(solution)/shard_map/ppermute | solution.py:473
  355.4 25.9 %collective-permute-start.23 = (f32[4,2,256,128]{3,2,1,0:T(8,128)}, f32[4,2,256,128]{3,2,1,0:T(8,128)S(1)}, u32[]{:S(2)}, u32[]{:S(2)}) collective-permute-start(f32[4,2,256,128]{3,2,1,0:T(8,128)} %slice.107), channel_id=1, source_target_pairs={{0,32},{4,36},{8,40},{12,44},{16,48},{20,52},{24,56},{28,60},{32,6... | collective-permute-start | bytes 3145736 | tf_op jit(solution)/shard_map/ppermute | solution.py:472
  360.5 25.4 %collective-permute-start.29 = (f32[4,2,256,128]{3,2,1,0:T(8,128)}, f32[4,2,256,128]{3,2,1,0:T(8,128)}, u32[]{:S(2)}, u32[]{:S(2)}) collective-permute-start(f32[4,2,256,128]{3,2,1,0:T(8,128)} %slice.110), channel_id=1, source_target_pairs={{0,24},{4,28},{8,0},{12,4},{16,8},{20,12},{24,16},{28,20},{32,56},... | collective-permute-start | bytes 3145736 | tf_op jit(solution)/shard_map/ppermute | solution.py:473
  365.4 26.3 %collective-permute-start.27 = (f32[4,2,256,128]{3,2,1,0:T(8,128)}, f32[4,2,256,128]{3,2,1,0:T(8,128)}, u32[]{:S(2)}, u32[]{:S(2)}) collective-permute-start(f32[4,2,256,128]{3,2,1,0:T(8,128)} %slice.109), channel_id=1, source_target_pairs={{0,8},{4,12},{8,16},{12,20},{16,24},{20,28},{24,0},{28,4},{32,40},... | collective-permute-start | bytes 3145736 | tf_op jit(solution)/shard_map/ppermute | solution.py:472
  (13 other events, 40.7 us)
Sparse Core Ops, SparseCore 0:
  170.3 57.7 all-gather.6
  229.7 71.0 all-gather.4
where the time goes:
time: 432 us; the launch traced here: 425 us
  Pallas kernels  179 us (41%)
  waiting for transfers between devices  121 us (28%)
  starting transfers between devices  42.6 us (10%)
  blocking collectives  26.6 us (6%)
  other arithmetic  21.3 us (5%)
  local copies, waits for them, and re-layouts  19.9 us (5%)
  between operations  14.3 us (3%)
    pallas_call x1, Pallas kernels, factor(): pl.pallas_call(factor_kernel, out_shape=(whole, whole), in_specs=[SM, VM,...  101 us
    ppermute x13, waiting for transfers between devices, moved(): return lax.ppermute(part, both, pairs)  54.9 us
    all_to_all x1, blocking collectives, shards(): lax.all_to_all(panel, 'row', split_axis=0, concat_axis=0, tiled=True)  26.6 us
    pallas_call x1, Pallas kernels, schur(): pl.pallas_call(schur_kernel, grid_spec=pltpu.PrefetchScalarGridSpec(num_s...  25.8 us
    all_gather x2, waiting for transfers between devices, gathered(): return lax.all_gather(value, 'row', axis_index_groups=groups)  23.2 us
    ppermute x2, waiting for transfers between devices, across(): return jnp.stack([value, lax.ppermute(value, axis, pairs)])  19.4 us
    pallas_call x1, Pallas kernels, build_head(): pl.pallas_call(head_kernel, out_shape=(jax.ShapeDtypeStruct((32 * 72, 128...  14.3 us
    ppermute x13, starting transfers between devices, moved(): return lax.ppermute(part, both, pairs)  14.2 us
  transfers between devices with their start and end apart: 33, of which 10 were waited for; matrix products, arithmetic and copies ran while one was open for 6% of the time, Pallas kernels for 31%

commit v1 on v0

--- a/solution.py
+++ b/solution.py
@@ -1,5 +1,6 @@
 import jax
 import jax.numpy as jnp
+import numpy as np
 from jax import lax
 from jax.experimental import pallas as pl
 from jax.experimental.pallas import tpu as pltpu
@@ -302,7 +303,7 @@
     )(pos, corner_lo, corner_hi)
 
 
-def left_kernel(pos_ref, a_ref, x_ref, head_ref, w_ref, wide, rows):
+def left_kernel(pos_ref, a_ref, x_ref, head_ref, kept_ref, given_ref, wide, rows):
     my_row, my_col = pos_ref[0], pos_ref[1]
     for far in range(2):
         for core in range(2):
@@ -313,15 +314,17 @@
         rows[:, here] = dot_nt(wide[:, :(b + 1) * 256], x_ref[here, :(b + 1) * 256])
     for b in range(4):
         here = slice(b * 256, (b + 1) * 256)
-        w_ref[:, here] = dot_nn(rows[:, b * 256:], x_ref[b * 256:, here])
+        product = dot_nn(rows[:, b * 256:], x_ref[b * 256:, here])
+        kept_ref[:, here] = product
+        given_ref[:, here] = product
 
     @pl.when(my_row < 4)
     def _():
         rows[...] = head_ref[...]
 
-    for core in range(2):
+    for core, ref in enumerate((kept_ref, given_ref)):
         column = pl.multiple_of(jnp.bitwise_xor(my_col, core) * 256, 256)
-        w_ref[:, 1024 + core * 256:1280 + core * 256] = rows[:, pl.ds(column, 256)]
+        ref[:, 1024:] = rows[:, pl.ds(column, 256)]
 
 
 def left(pos, a, inverse, lower):
@@ -335,10 +338,10 @@
                 pl.BlockSpec((1024, 1024), lambda i, pos: (0, 0)),
                 pl.BlockSpec((256, 1024), lambda i, pos: (jnp.minimum(pos[0], 3), 0)),
             ],
-            out_specs=pl.BlockSpec((256, 1536), lambda i, pos: (0, 0)),
+            out_specs=(pl.BlockSpec((256, 1280), lambda i, pos: (0, 0)),) * 2,
             scratch_shapes=[pltpu.VMEM((256, 1024), F32), pltpu.VMEM((256, 1024), F32)],
         ),
-        out_shape=jax.ShapeDtypeStruct((256, 1536), F32),
+        out_shape=(jax.ShapeDtypeStruct((256, 1280), F32),) * 2,
         compiler_params=params(),
         cost_estimate=pl.CostEstimate(flops=10**6, bytes_accessed=2**12, transcendentals=0),
     )(pos, a, inverse, lower)
@@ -353,7 +356,7 @@
     return lax.dot_general(a, b, (((1,), (0,)), ((), ())), preferred_element_type=F32)
 
 
-def schur_kernel(table_ref, front_ref, w_ref, *refs):
+def schur_kernel(table_ref, front_ref, kept_ref, got_ref, *refs):
     out_ref, partial, w_high, w_low = refs[10:]
     f, j = pl.program_id(0), pl.program_id(1)
     my_row = table_ref[144]
@@ -369,10 +372,12 @@
         for h in range(2):
             out_ref[0, places[h], :] = value[:, h * 128:(h + 1) * 128]
 
-    @pl.when(j == 0)
-    def _():
-        put(w_ref[0, :, 1024:1280])
-        w_high[...], w_low[...] = split(w_ref[0, :, :1024])
+    for other, ref in enumerate((kept_ref, got_ref)):
+
+        @pl.when((j == 0) & (jnp.bitwise_xor(f, table_ref[128]) == other))
+        def _():
+            put(ref[:, 1024:])
+            w_high[...], w_low[...] = split(ref[:, :1024])
 
     for part in range(2):
         own, below, first, second, above = refs[5 * part:5 * part + 5]
@@ -408,20 +413,23 @@
 
 
 def schur_steps(pos):
-    step = jnp.arange(16, dtype=jnp.int32)
-    x, z = step // 4, (pos[1] + 4 - step % 4) % 4
-    my_x, my_z = pos[0] // 8, (pos[0] // 2) % 4
-    rows = [(my_x + 4 - x) % 4, (my_z + 4 - z) % 4]
-    for k in (0, 1, 2, 2, 3):
-        mine = (my_x + 4 - k) % 4
-        idle = jnp.where(x < mine, z[0], z[3])
-        rows.append(jnp.where(x == mine, z, idle))
-    rows.append(x)
-    rows.append(jnp.broadcast_to(pos[1] % 2, (16,)))
-    return jnp.concatenate([jnp.concatenate(rows), pos]).astype(jnp.int32)
-
-
-def schur(pos, front, w, lo, hi):
+    line, step = np.repeat(np.arange(10), 16).astype(np.int32), np.tile(np.arange(16), 10).astype(np.int32)
+    turns = np.repeat(np.array([0, 0, 0, 1, 2, 2, 3, 0, 0, 0], np.int32), 16)
+    x = step // 4
+    my_row, my_col = pos[0], pos[1]
+    my_x, my_z = my_row // 8, jnp.bitwise_and(my_row // 2, 3)
+    z = jnp.bitwise_and(my_col + 4 - step % 4, 3)
+    mine = jnp.bitwise_and(my_x + 4 - turns, 3)
+    idle = jnp.where(x < mine, my_col, jnp.bitwise_and(my_col + 1, 3))
+    value = jnp.where(step == 0, my_row, my_col)
+    value = jnp.where(line == 8, jnp.bitwise_and(my_col, 1), value)
+    value = jnp.where(line == 7, x, value)
+    value = jnp.where(line < 7, jnp.where(x == mine, z, idle), value)
+    value = jnp.where(line == 1, jnp.bitwise_and(my_z + 4 - z, 3), value)
+    return jnp.where(line == 0, jnp.bitwise_and(my_x + 4 - x, 3), value).astype(jnp.int32)
+
+
+def schur(table, front, kept, got, lo, hi):
     def lo_map(row):
         return lambda f, j, table: (table[row * 16 + f * 8 + j], 0, 0, 0)
 
@@ -436,9 +444,8 @@
             grid=(2, 8),
             in_specs=[
                 pl.BlockSpec((1, 4096, 128), fixed),
-                pl.BlockSpec(
-                    (1, 256, 1280), lambda f, j, table: (jnp.bitwise_xor(f, table[128]), 0, 0)
-                ),
+                pl.BlockSpec((256, 1280), lambda f, j, table: (0, 0)),
+                pl.BlockSpec((256, 1280), lambda f, j, table: (0, 0)),
             ]
             + [pl.BlockSpec((1, 2, n, 128), lo_map(2 + i)) for i, n in enumerate(rows)]
             + [pl.BlockSpec((1, 2, n, 128), lo_map(7)) for n in rows],
@@ -451,7 +458,7 @@
         ),
         out_shape=jax.ShapeDtypeStruct((2, 4096, 128), F32),
         compiler_params=params(),
-    )(schur_steps(pos), front, w, *lo, *hi)
+    )(table, front, kept, got, *lo, *hi)
 
 
 def turn(axis, by):
@@ -464,13 +471,14 @@
     return pairs
 
 
-def ring(value, axis):
-    forth, back = turn(axis, 1), turn(axis, -1)
+def ring_near(value, axis):
+    return lax.ppermute(value, "row", turn(axis, 1)), lax.ppermute(value, "row", turn(axis, -1))
+
+
+def ring(value, below, above, axis):
     half = value.shape[-2] // 2
-    below = lax.ppermute(value, "row", forth)
-    above = lax.ppermute(value, "row", back)
-    first = lax.ppermute(below[..., :half, :], "row", forth)
-    second = lax.ppermute(above[..., half:, :], "row", back)
+    first = lax.ppermute(below[..., :half, :], "row", turn(axis, 1))
+    second = lax.ppermute(above[..., half:, :], "row", turn(axis, -1))
     return value, below, first, second, above
 
 
@@ -488,7 +496,6 @@
 
 CORE = [(0, 1), (1, 0), (2, 3), (3, 2)]
 FAR = [(0, 2), (2, 0), (1, 3), (3, 1)]
-NEAR = [(i, i ^ 1) for i in range(32)]
 
 
 def own_front(value, my_core):
@@ -501,7 +508,7 @@
     return (x * 8 + z * 2 + y % 2) * 4 + (y // 2) * 2 + core
 
 
-def corner_columns(piece, moved, my_x, my_z, my_y, my_core):
+def corner_columns(piece, moved, near, my_x, my_z, my_y, my_core):
     both = ("row", "col")
     got = []
     for k in range(4):
@@ -510,7 +517,7 @@
             for f in range(2) for z in range(4) for h in range(2)
         ]
         got.append(lax.ppermute(piece, both, pairs))
-    got, moved = lax.optimization_barrier((got, moved))
+    got, moved, near = lax.optimization_barrier((got, moved, near))
     got = jnp.stack(got)
     pair = jnp.stack(
         [lax.dynamic_index_in_dim(got, (my_y + 4 - h) % 4, 0, keepdims=False) for h in range(2)]
@@ -548,9 +555,8 @@
 
     lo = ring_z(pair[:, :LOW], lambda core: [2 * core])
     hi = spread_x(pair[:, LOW:])
-    near = across(moved, NEAR, "row")
-    lo, hi, near = lax.optimization_barrier((lo, hi, near))
-    return spread_x(lo), ring_z(hi, lambda core: range(4)), near
+    lo, hi = lax.optimization_barrier((lo, hi))
+    return spread_x(lo), ring_z(hi, lambda core: range(4)), jnp.stack([moved, near])
 
 
 def shards(contrib, target_rows, diag_shift, pattern):
@@ -570,26 +576,26 @@
     piece = panel_piece(pos, marks, pattern, panel.reshape(32 * 72, 128))
     slots, piece = lax.optimization_barrier((slots, piece))
     main = build_main(slots, contrib)
-    moves = [
-        (i * 4 + c, i * 4 + ((i // 2) % 4 + c) % 4) for i in range(32) for c in range(4)
-    ]
-    moved = lax.ppermute(piece, ("row", "col"), moves)
-    corner_lo, corner_hi, pair = corner_columns(piece, moved, my_x, my_z, my_y, my_core)
-    corner_lo, corner_hi, main, pair = lax.optimization_barrier((corner_lo, corner_hi, main, pair))
-    lo, hi = gathered(pair[:, :512], "z"), gathered(pair[:, 512:], "x")
+    places = [(i, c, ((i // 2) % 4 + c) % 4) for i in range(32) for c in range(4)]
+    moved = lax.ppermute(piece, ("row", "col"), [(i * 4 + c, i * 4 + to) for i, c, to in places])
+    near = lax.ppermute(piece, ("row", "col"), [(i * 4 + c, (i ^ 1) * 4 + to) for i, c, to in places])
+    corner_lo, corner_hi, pair = corner_columns(piece, moved, near, my_x, my_z, my_y, my_core)
+    lo = gathered(pair[:, :512], "z")
+    corner_lo, corner_hi, main, pair, table = lax.optimization_barrier(
+        (corner_lo, corner_hi, main, pair, schur_steps(pos))
+    )
+    hi = gathered(pair[:, 512:], "x")
     main = lax.all_to_all(
         main.reshape(128, 128, 128), ("row", "col"), split_axis=0, concat_axis=0, tiled=True
     )
     lower, inverse = factor(pos, corner_lo, corner_hi)
     main, lower, lo, hi = lax.optimization_barrier((main, lower, lo, hi))
-    lo, hi = ring(lo, "x"), ring(hi, "z")
+    lo_near, hi_near = ring_near(lo, "x"), ring_near(hi, "z")
     front, own_left = assemble(pos, marks, pattern, diag, main.reshape(16384, 128))
     lefts = own_front(own_left, my_core)
-    w = left(pos, lefts, inverse, lower)
-    kept = w[:, :1280]
-    given = jnp.concatenate([w[:, :1024], w[:, 1280:]], axis=1)
-    w = jnp.stack([kept, lax.ppermute(given, "col", CORE)])
-    result = schur(pos, front, w, lo, hi)
+    lo, hi = ring(lo, *lo_near, "x"), ring(hi, *hi_near, "z")
+    kept, given = left(pos, lefts, inverse, lower)
+    result = schur(table, front, kept, lax.ppermute(given, "col", CORE), lo, hi)
     return result.reshape(2, 1, 1, 256, 8, 1, 256)
 
 

time: 432 us -> 430 us (level)
  starting transfers between devices: 42.6 us -> 56.6 us
  waiting for transfers between devices: 121 us -> 114 us
  other arithmetic: 21.3 us -> 16 us
    all_gather x2, waiting for transfers between devices: 23.2 us -> 0.01 us  [gathered(): return lax.all_gather(value, 'row', axis_index_groups=groups)]
    all_to_all x1, starting transfers between devices: 5.96 us -> 23.5 us  [shards(): lax.all_to_all(main.reshape(128, 128, 128), ('row', 'col'), split_axis=0,...]
    all_to_all x1, waiting for transfers between devices: 0.01 us -> 13.8 us  [shards(): lax.all_to_all(main.reshape(128, 128, 128), ('row', 'col'), split_axis=0,...]
    ppermute x10 -> x11, waiting for transfers between devices: 21.1 us -> 33.7 us  [the longest x2 19.5 us: ring(): second = lax.ppermute(above[..., half:, :], 'row', turn(axis, -1))]
    slice x10 -> x5, local copies, waits for them, and re-layouts: 11 us -> 5.37 us  [the longest x2 3.19 us: ring(): first = lax.ppermute(below[..., :half, :], 'row', turn(axis, 1))]
    ppermute x13, waiting for transfers between devices: 54.9 us -> 49.5 us  [moved(): return lax.ppermute(part, both, pairs)]
    ppermute x2 -> x1, waiting for transfers between devices: 19.4 us -> 15.5 us  [across(): return jnp.stack([value, lax.ppermute(value, axis, pairs)])]
    ppermute x10 -> x11, starting transfers between devices: 16 us -> 14.3 us  [the longest x2 6.7 us: ring_near(): lax.ppermute(value, 'row', turn(axis, 1))]
  transfers between devices with their start and end apart: 33 -> 33, of which waited for: 10 -> 11; matrix products, arithmetic and copies ran while one was open for 6% -> 5% of each run, Pallas kernels for 31% -> 31%
where the time goes in v1:
time: 430 us; the launch traced here: 423 us
  Pallas kernels  179 us (42%)
  waiting for transfers between devices  114 us (27%)
  starting transfers between devices  56.6 us (13%)
  blocking collectives  26.6 us (6%)
  local copies, waits for them, and re-layouts  16.2 us (4%)
  other arithmetic  16 us (4%)
  between operations  14.5 us (3%)
    pallas_call x1, Pallas kernels, factor(): pl.pallas_call(factor_kernel, out_shape=(whole, whole), in_specs=[SM, VM,...  100 us
    ppermute x13, waiting for transfers between devices, moved(): return lax.ppermute(part, both, pairs)  49.5 us
    all_to_all x1, blocking collectives, shards(): lax.all_to_all(panel, 'row', split_axis=0, concat_axis=0, tiled=True)  26.6 us
    pallas_call x1, Pallas kernels, schur(): pl.pallas_call(schur_kernel, grid_spec=pltpu.PrefetchScalarGridSpec(num_s...  25.6 us
    all_to_all x1, starting transfers between devices, shards(): lax.all_to_all(main.reshape(128, 128, 128), ('row', 'col'), split_axis=0,...  23.5 us
    ppermute x2, waiting for transfers between devices, ring(): second = lax.ppermute(above[..., half:, :], 'row', turn(axis, -1))  19.5 us
    ppermute x1, waiting for transfers between devices, across(): return jnp.stack([value, lax.ppermute(value, axis, pairs)])  15.5 us
    ppermute x13, starting transfers between devices, moved(): return lax.ppermute(part, both, pairs)  15.4 us
  transfers between devices with their start and end apart: 33, of which 11 were waited for; matrix products, arithmetic and copies ran while one was open for 5% of the time, Pallas kernels for 31%

profile of v1, /device:TPU:6, one launch (start us, length us, event | category | flops | bytes accessed | tf_op | source)
XLA Modules:
  0.0 423.3 jit_solution(14125865219478925880)
XLA Ops:
  7.2 14.3 %shard_map.127 = (f32[2304,128]{1,0:T(8,128)}, s32[32,32]{1,0:T(8,128)}, s32[2,256]{1,0:T(2,128)}) custom-call(s32[2]{0:T(128)} %pad_add_fusion.pos_ref, s32[2,256]{1,0:T(2,128)} %t_ref.1, f32[2,256,2048]{2,1,0:T(8,128)} %x_ref.3, f32[2,2,128]{2,1,0:T(2,128)} %bitcast.68), custom_call_target="tpu_custom_call" | custom-call | tf_op jit(solution)/shard_map/pallas_call | solution.py:75
  24.9 26.6 %all_to_all.10 = f32[32,72,128]{2,1,0:T(8,128)S(1)} all-to-all(f32[32,72,128]{2,1,0:T(8,128)} %scatter.4), channel_id=1, replica_groups=mesh['row'=32,'col'=4] {'row'}, dimensions={0} | all-to-all | bytes 2359296 | tf_op jit(solution)/shard_map/all_to_all | solution.py:574
  52.4 7.6 %shard_map.128 = f32[1024,128]{1,0:T(8,128)} custom-call(s32[2]{0:T(128)} %pad_add_fusion.pos_ref, s32[32,96]{1,0:T(8,128)} %convert_bitcast_fusion.marks_ref, s32[2,32]{1,0:T(2,128)} %pattern_ref.3, f32[2304,128]{1,0:T(8,128)} %bitcast.43), custom_call_target="tpu_custom_call" | custom-call | tf_op jit(solution)/shard_map/pallas_call | solution.py:156
  60.9 1.7 collective-permute-start.4
  64.7 8.6 %collective-permute-done.5 = f32[1024,128]{1,0:T(8,128)} collective-permute-done((f32[1024,128]{1,0:T(8,128)}, f32[1024,128]{1,0:T(8,128)}, u32[]{:S(2)}, u32[]{:S(2)}) %collective-permute-start.5) | collective-permute-done | bytes 524320 | tf_op jit(solution)/shard_map/ppermute | solution.py:581
  84.1 26.2 %collective-permute-done.10 = f32[2,640,128]{2,1,0:T(8,128)} collective-permute-done((f32[2,640,128]{2,1,0:T(8,128)S(1)}, f32[2,640,128]{2,1,0:T(8,128)}, u32[]{:S(2)}, u32[]{:S(2)}) %collective-permute-start.10) | collective-permute-done | bytes 655392 | tf_op jit(solution)/shard_map/ppermute | solution.py:535
  112.8 1.8 collective-permute-start.12
  114.6 1.8 fusion.2
  117.1 2.0 collective-permute-start.16
  119.1 23.3 %collective-permute-done.13 = f32[4,2,384,128]{3,2,1,0:T(8,128)} collective-permute-done((f32[4,2,384,128]{3,2,1,0:T(8,128)S(1)}, f32[4,2,384,128]{3,2,1,0:T(8,128)}, u32[]{:S(2)}, u32[]{:S(2)}) %collective-permute-start.13) | collective-permute-done | bytes 1572896 | tf_op jit(solution)/shard_map/ppermute | solution.py:535
  142.4 2.1 slice.75
  144.5 2.2 collective-permute-start.15
  146.7 2.1 slice.74
  150.5 9.5 %shard_map.129 = f32[16384,128]{1,0:T(8,128)} custom-call(s32[2,256]{1,0:T(2,128)} %get-tuple-element.55.slots_ref, f32[2,256,2048]{2,1,0:T(8,128)} %x_ref.3), custom_call_target="tpu_custom_call" | custom-call | flops 10000000000 | bytes 8388608 | tf_op jit(solution)/shard_map/pallas_call | solution.py:108
  161.2 3.2 pad_maximum_fusion.hi_ref
  164.4 3.4 fusion.1.lo_ref
  167.7 23.5 %all-to-all-start.1 = ((f32[128,128,128]{2,1,0:T(8,128)}), f32[128,128,128]{2,1,0:T(8,128)}, u32[]{:S(2)}, u32[]{:S(2)}) async-start(f32[128,128,128]{2,1,0:T(8,128)} %bitcast.42), calls=%async_computation.1 | async-start | bytes 16777216 | tf_op jit(solution)/shard_map/all_to_all | solution.py:588
  192.3 100.5 %shard_map.130 = (f32[1024,1024]{1,0:T(8,128)}, f32[1024,1024]{1,0:T(8,128)}) custom-call(s32[2]{0:T(128)} %pad_add_fusion.pos_ref, f32[4,2,384,128]{3,2,1,0:T(8,128)} %fusion.1.lo_ref, f32[4,2,640,128]{3,2,1,0:T(8,128)} %pad_maximum_fusion.hi_ref), custom_call_target="tpu_custom_call" | custom-call | flops 99999997952 | bytes 12582912 | tf_op jit(solution)/shard_map/pallas_call | solution.py:295
  292.8 13.8 %all-to-all-done.1 = f32[128,128,128]{2,1,0:T(8,128)} async-done(((f32[128,128,128]{2,1,0:T(8,128)}), f32[128,128,128]{2,1,0:T(8,128)}, u32[]{:S(2)}, u32[]{:S(2)}) %all-to-all-start.1) | async-done | bytes 8388640 | tf_op jit(solution)/shard_map/all_to_all | solution.py:588
  306.7 4.7 %collective-permute-start.22 = (f32[4,2,512,128]{3,2,1,0:T(8,128)}, f32[4,2,512,128]{3,2,1,0:T(8,128)}, u32[]{:S(2)}, u32[]{:S(2)}) collective-permute-start(f32[4,2,512,128]{3,2,1,0:T(8,128)} %bitcast.48), channel_id=1, source_target_pairs={{0,32},{4,36},{8,40},{12,44},{16,48},{20,52},{24,56},{28,60},{32,6... | collective-permute-start | bytes 6291464 | tf_op jit(solution)/shard_map/ppermute | solution.py:475
  311.4 2.0 collective-permute-start.26
  313.5 11.9 %shard_map.131 = (f32[2,4096,128]{2,1,0:T(8,128)}, f32[2,256,256]{2,1,0:T(8,128)}) custom-call(s32[2]{0:T(128)} %pad_add_fusion.pos_ref, s32[32,96]{1,0:T(8,128)} %convert_bitcast_fusion.marks_ref, s32[2,32]{1,0:T(2,128)} %pattern_ref.3, f32[2,2,128]{2,1,0:T(2,128)} %bitcast.69, f32[16384,128]{1,0:T(8,128)} %bitcast.29.x_ref), custom_call_target="tpu_custom_call" | custom-call | flops 1000000 | bytes 4096 | tf_op jit(solution)/shard_map/pallas_call | solution.py:212
  328.5 15.5 %collective-permute-done.20 = f32[2,256,256]{2,1,0:T(8,128)S(1)} collective-permute-done((f32[2,256,256]{2,1,0:T(8,128)S(1)}, f32[2,256,256]{2,1,0:T(8,128)S(1)}, u32[]{:S(2)}, u32[]{:S(2)}) %collective-permute-start.20) | collective-permute-done | bytes 524320 | tf_op jit(solution)/shard_map/ppermute | solution.py:494
  345.0 9.9 %shard_map.132 = (f32[256,1280]{1,0:T(8,128)}, f32[256,1280]{1,0:T(8,128)}) custom-call(s32[2]{0:T(128)} %pad_add_fusion.pos_ref, f32[2,2,256,256]{3,2,1,0:T(8,128)} %pad_maximum_fusion.4.a_ref, f32[1024,1024]{1,0:T(8,128)} %get-tuple-element.67.x_ref, f32[1024,1024]{1,0:T(8,128)} %get-tuple-element.68.head_ref), custom_call_target="tpu_custom_call" | custom-call | flops 1000000 | bytes 4096 | tf_op jit(solution)/shard_map/pallas_call | solution.py:331
  354.9 2.1 collective-permute-done.24.refs_4_
  357.2 1.9 slice.78
  359.1 2.7 collective-permute-start.23
  364.5 2.1 collective-permute-start.27
  366.6 16.1 %collective-permute-done.25.refs_3_ = f32[4,2,256,128]{3,2,1,0:T(8,128)} collective-permute-done((f32[4,2,256,128]{3,2,1,0:T(8,128)S(1)}, f32[4,2,256,128]{3,2,1,0:T(8,128)}, u32[]{:S(2)}, u32[]{:S(2)}) %collective-permute-start.25) | collective-permute-done | bytes 1048608 | tf_op jit(solution)/shard_map/ppermute | solution.py:481
  383.5 3.3 collective-permute-done.29.refs_8_
  386.9 2.6 collective-permute-done.27.refs_7_
  390.5 25.6 %shard_map.133 = f32[2,4096,128]{2,1,0:T(8,128)} custom-call(s32[160]{0:T(256)} %fusion.5.table_ref, f32[2,4096,128]{2,1,0:T(8,128)} %get-tuple-element.65.front_ref, f32[256,1280]{1,0:T(8,128)} %get-tuple-element.69.kept_ref, f32[256,1280]{1,0:T(8,128)} %copy-done.5, f32[4,2,512,128]{3,2,1,0:T(8,128)} %bitcast.49, ...), custom_call_target="tpu_custom_call" | custom-call | tf_op jit(solution)/shard_map/pallas_call | solution.py:440
  (118 shorter events, 34.1 us)
Async XLA Ops:
  6.5 286.3 %all-gather.5.cloned.1.call-start = ((), (), s32[]{:S(2)}) async-start(), calls=%async_computation.2 | async-start | bytes 2621440 | tf_op jit(solution)/shard_map/all_gather | solution.py:490
  60.0 13.3 %collective-permute-start.5 = (f32[1024,128]{1,0:T(8,128)}, f32[1024,128]{1,0:T(8,128)}, u32[]{:S(2)}, u32[]{:S(2)}) collective-permute-start(f32[1024,128]{1,0:T(8,128)} %shard_map.128), channel_id=1, source_target_pairs={{0,4},{1,5},{2,6},{3,7},{4,0},{5,1},{6,2},{7,3},{8,13},{9,14},{10,... | collective-permute-start | bytes 1572872 | tf_op jit(solution)/shard_map/ppermute | solution.py:581
  60.9 13.2 %collective-permute-start.4 = (f32[1024,128]{1,0:T(8,128)}, f32[1024,128]{1,0:T(8,128)S(1)}, u32[]{:S(2)}, u32[]{:S(2)}) collective-permute-start(f32[1024,128]{1,0:T(8,128)} %shard_map.128), channel_id=1, source_target_pairs={{0,0},{1,1},{2,2},{3,3},{4,4},{5,5},{6,6},{7,7},{8,9},{9,10},{10,1... | collective-permute-start | bytes 1572872 | tf_op jit(solution)/shard_map/ppermute | solution.py:580
  62.6 11.5 %collective-permute-start.3 = (f32[1024,128]{1,0:T(8,128)}, f32[1024,128]{1,0:T(8,128)S(1)}, u32[]{:S(2)}, u32[]{:S(2)}) collective-permute-start(f32[1024,128]{1,0:T(8,128)} %shard_map.128), channel_id=1, source_target_pairs={{0,6},{4,0},{8,14},{12,8},{16,22},{20,16},{24,30},{28,24},{64,71},... | collective-permute-start | bytes 1572872 | tf_op jit(solution)/shard_map/ppermute | solution.py:519
  63.3 10.8 %collective-permute-start.2 = (f32[1024,128]{1,0:T(8,128)}, f32[1024,128]{1,0:T(8,128)S(1)}, u32[]{:S(2)}, u32[]{:S(2)}) collective-permute-start(f32[1024,128]{1,0:T(8,128)} %shard_map.128), channel_id=1, source_target_pairs={{0,2},{4,6},{8,10},{12,14},{16,18},{20,22},{24,26},{28,30},{64,67}... | collective-permute-start | bytes 1572872 | tf_op jit(solution)/shard_map/ppermute | solution.py:519
  64.0 10.2 %collective-permute-start.1 = (f32[1024,128]{1,0:T(8,128)}, f32[1024,128]{1,0:T(8,128)S(1)}, u32[]{:S(2)}, u32[]{:S(2)}) collective-permute-start(f32[1024,128]{1,0:T(8,128)} %shard_map.128), channel_id=1, source_target_pairs={{0,4},{4,2},{8,12},{12,10},{16,20},{20,18},{24,28},{28,26},{64,69}... | collective-permute-start | bytes 1572872 | tf_op jit(solution)/shard_map/ppermute | solution.py:519
  73.3 0.8 collective-permute-start
  75.2 5.8 %collective-permute-start.7 = (f32[2,384,128]{2,1,0:T(8,128)S(1)}, f32[2,384,128]{2,1,0:T(8,128)S(1)}, u32[]{:S(2)}, u32[]{:S(2)}) collective-permute-start(f32[2,384,128]{2,1,0:T(8,128)S(1)} %pad_maximum_fusion.7), channel_id=1, source_target_pairs={{0,16},{65,81},{4,20},{69,85},{2,18},{67,83},{6,22},{71,87},{8,24}... | collective-permute-start | bytes 1179656 | tf_op jit(solution)/shard_map/ppermute | solution.py:552
  75.9 34.3 %collective-permute-start.10 = (f32[2,640,128]{2,1,0:T(8,128)S(1)}, f32[2,640,128]{2,1,0:T(8,128)}, u32[]{:S(2)}, u32[]{:S(2)}) collective-permute-start(f32[2,640,128]{2,1,0:T(8,128)S(1)} %pad_maximum_fusion.5), channel_id=1, source_target_pairs={{0,96},{65,33},{4,100},{69,37},{2,98},{67,35},{6,102},{71,39},{8,1... | collective-permute-start | bytes 1966088 | tf_op jit(solution)/shard_map/ppermute | solution.py:535
  77.2 33.0 %collective-permute-start.9 = (f32[2,640,128]{2,1,0:T(8,128)S(1)}, f32[2,640,128]{2,1,0:T(8,128)}, u32[]{:S(2)}, u32[]{:S(2)}) collective-permute-start(f32[2,640,128]{2,1,0:T(8,128)S(1)} %pad_maximum_fusion.5), channel_id=1, source_target_pairs={{0,32},{65,97},{4,36},{69,101},{2,34},{67,99},{6,38},{71,103},{8,4... | collective-permute-start | bytes 1966088 | tf_op jit(solution)/shard_map/ppermute | solution.py:535
  78.8 31.5 %collective-permute-start.11 = (f32[2,640,128]{2,1,0:T(8,128)S(1)}, f32[2,640,128]{2,1,0:T(8,128)}, u32[]{:S(2)}, u32[]{:S(2)}) collective-permute-start(f32[2,640,128]{2,1,0:T(8,128)S(1)} %pad_maximum_fusion.5), channel_id=1, source_target_pairs={{0,64},{65,1},{4,68},{69,5},{2,66},{67,3},{6,70},{71,7},{8,72},{73... | collective-permute-start | bytes 1966088 | tf_op jit(solution)/shard_map/ppermute | solution.py:535
  80.2 1.5 collective-permute-start.6
  111.5 31.0 %collective-permute-start.13 = (f32[4,2,384,128]{3,2,1,0:T(8,128)S(1)}, f32[4,2,384,128]{3,2,1,0:T(8,128)}, u32[]{:S(2)}, u32[]{:S(2)}) collective-permute-start(f32[4,2,384,128]{3,2,1,0:T(8,128)S(1)} %pad_maximum_fusion.2), channel_id=1, source_target_pairs={{0,96},{65,33},{4,100},{69,37},{2,98},{67,35},{6,102},{71,39},{8,1... | collective-permute-start | bytes 4718600 | tf_op jit(solution)/shard_map/ppermute | solution.py:535
  112.8 33.9 %collective-permute-start.12 = (f32[4,2,384,128]{3,2,1,0:T(8,128)S(1)}, f32[4,2,384,128]{3,2,1,0:T(8,128)}, u32[]{:S(2)}, u32[]{:S(2)}) collective-permute-start(f32[4,2,384,128]{3,2,1,0:T(8,128)S(1)} %pad_maximum_fusion.2), channel_id=1, source_target_pairs={{0,32},{65,97},{4,36},{69,101},{2,34},{67,99},{6,38},{71,103},{8,4... | collective-permute-start | bytes 4718600 | tf_op jit(solution)/shard_map/ppermute | solution.py:535
  117.1 44.1 %collective-permute-start.18 = (f32[2,640,128]{2,1,0:T(8,128)S(1)}, f32[2,640,128]{2,1,0:T(8,128)}, u32[]{:S(2)}, u32[]{:S(2)}) collective-permute-start(f32[2,640,128]{2,1,0:T(8,128)S(1)} %select_select_fusion), channel_id=1, source_target_pairs={{0,24},{32,56},{64,88},{96,120},{1,25},{33,57},{65,89},{97,121},{4... | collective-permute-start | bytes 1966088 | tf_op jit(solution)/shard_map/ppermute | solution.py:552
  117.1 44.1 %collective-permute-start.17 = (f32[2,640,128]{2,1,0:T(8,128)S(1)}, f32[2,640,128]{2,1,0:T(8,128)}, u32[]{:S(2)}, u32[]{:S(2)}) collective-permute-start(f32[2,640,128]{2,1,0:T(8,128)S(1)} %select_select_fusion), channel_id=1, source_target_pairs={{0,16},{32,48},{64,80},{96,112},{1,17},{33,49},{65,81},{97,113},{4... | collective-permute-start | bytes 1966088 | tf_op jit(solution)/shard_map/ppermute | solution.py:552
  117.1 44.1 %collective-permute-start.16 = (f32[2,640,128]{2,1,0:T(8,128)S(1)}, f32[2,640,128]{2,1,0:T(8,128)}, u32[]{:S(2)}, u32[]{:S(2)}) collective-permute-start(f32[2,640,128]{2,1,0:T(8,128)S(1)} %select_select_fusion), channel_id=1, source_target_pairs={{0,8},{32,40},{64,72},{96,104},{1,9},{33,41},{65,73},{97,105},{4,1... | collective-permute-start | bytes 1966088 | tf_op jit(solution)/shard_map/ppermute | solution.py:552
  144.5 19.9 %collective-permute-start.15 = (f32[4,2,192,128]{3,2,1,0:T(8,128)}, f32[4,2,192,128]{3,2,1,0:T(8,128)}, u32[]{:S(2)}, u32[]{:S(2)}) collective-permute-start(f32[4,2,192,128]{3,2,1,0:T(8,128)} %slice.75), channel_id=1, source_target_pairs={{96,64},{33,1},{100,68},{37,5},{98,66},{35,3},{102,70},{39,7},{104... | collective-permute-start | bytes 2359304 | tf_op jit(solution)/shard_map/ppermute | solution.py:535
  148.8 15.6 %collective-permute-start.14 = (f32[4,2,192,128]{3,2,1,0:T(8,128)}, f32[4,2,192,128]{3,2,1,0:T(8,128)}, u32[]{:S(2)}, u32[]{:S(2)}) collective-permute-start(f32[4,2,192,128]{3,2,1,0:T(8,128)} %slice.74), channel_id=1, source_target_pairs={{32,64},{97,1},{36,68},{101,5},{34,66},{99,3},{38,70},{103,7},{40,... | collective-permute-start | bytes 2359304 | tf_op jit(solution)/shard_map/ppermute | solution.py:535
  167.7 138.9 %all-to-all-start.1 = ((f32[128,128,128]{2,1,0:T(8,128)}), f32[128,128,128]{2,1,0:T(8,128)}, u32[]{:S(2)}, u32[]{:S(2)}) async-start(f32[128,128,128]{2,1,0:T(8,128)} %bitcast.42), calls=%async_computation.1 | async-start | bytes 16777216 | tf_op jit(solution)/shard_map/all_to_all | solution.py:588
  191.2 101.6 %all-gather.7.cloned.1.call-start = ((), (), s32[]{:S(2)}) async-start(), calls=%async_computation.3 | async-start | bytes 2621440 | tf_op jit(solution)/shard_map/all_gather | solution.py:490
  306.6 50.4 %collective-permute-start.24 = (f32[4,2,512,128]{3,2,1,0:T(8,128)}, f32[4,2,512,128]{3,2,1,0:T(8,128)S(1)}, u32[]{:S(2)}, u32[]{:S(2)}) collective-permute-start(f32[4,2,512,128]{3,2,1,0:T(8,128)} %bitcast.47), channel_id=1, source_target_pairs={{0,96},{4,100},{8,104},{12,108},{16,112},{20,116},{24,120},{28,124... | collective-permute-start | bytes 6291464 | tf_op jit(solution)/shard_map/ppermute | solution.py:475
  306.7 50.5 %collective-permute-start.22 = (f32[4,2,512,128]{3,2,1,0:T(8,128)}, f32[4,2,512,128]{3,2,1,0:T(8,128)}, u32[]{:S(2)}, u32[]{:S(2)}) collective-permute-start(f32[4,2,512,128]{3,2,1,0:T(8,128)} %bitcast.48), channel_id=1, source_target_pairs={{0,32},{4,36},{8,40},{12,44},{16,48},{20,52},{24,56},{28,60},{32,6... | collective-permute-start | bytes 6291464 | tf_op jit(solution)/shard_map/ppermute | solution.py:475
  311.4 50.4 %collective-permute-start.28 = (f32[4,2,512,128]{3,2,1,0:T(8,128)}, f32[4,2,512,128]{3,2,1,0:T(8,128)}, u32[]{:S(2)}, u32[]{:S(2)}) collective-permute-start(f32[4,2,512,128]{3,2,1,0:T(8,128)} %bitcast.50), channel_id=1, source_target_pairs={{0,24},{4,28},{8,0},{12,4},{16,8},{20,12},{24,16},{28,20},{32,56},... | collective-permute-start | bytes 6291464 | tf_op jit(solution)/shard_map/ppermute | solution.py:475
  311.4 51.8 %collective-permute-start.26 = (f32[4,2,512,128]{3,2,1,0:T(8,128)}, f32[4,2,512,128]{3,2,1,0:T(8,128)}, u32[]{:S(2)}, u32[]{:S(2)}) collective-permute-start(f32[4,2,512,128]{3,2,1,0:T(8,128)} %bitcast.51), channel_id=1, source_target_pairs={{0,8},{4,12},{8,16},{12,20},{16,24},{20,28},{24,0},{28,4},{32,40},... | collective-permute-start | bytes 6291464 | tf_op jit(solution)/shard_map/ppermute | solution.py:475
  326.5 1.6 collective-permute-start.19
  328.2 15.8 %collective-permute-start.20 = (f32[2,256,256]{2,1,0:T(8,128)S(1)}, f32[2,256,256]{2,1,0:T(8,128)S(1)}, u32[]{:S(2)}, u32[]{:S(2)}) collective-permute-start(f32[2,256,256]{2,1,0:T(8,128)S(1)} %get-tuple-element.76), channel_id=1, source_target_pairs={{0,2},{2,0},{1,3},{3,1},{4,6},{6,4},{5,7},{7,5},{8,10},{10,8},{9,1... | collective-permute-start | bytes 1572872 | tf_op jit(solution)/shard_map/ppermute | solution.py:494
  354.9 11.7 %collective-permute-start.21 = (f32[256,1280]{1,0:T(8,128)}, f32[256,1280]{1,0:T(8,128)S(1)}, u32[]{:S(2)}, u32[]{:S(2)}) collective-permute-start(f32[256,1280]{1,0:T(8,128)} %get-tuple-element.70), channel_id=1, source_target_pairs={{0,1},{1,0},{2,3},{3,2},{4,5},{5,4},{6,7},{7,6},{8,9},{9,8},{10,11... | collective-permute-start | bytes 3932168 | tf_op jit(solution)/shard_map/ppermute | solution.py:598
  357.1 25.6 %collective-permute-start.25 = (f32[4,2,256,128]{3,2,1,0:T(8,128)S(1)}, f32[4,2,256,128]{3,2,1,0:T(8,128)}, u32[]{:S(2)}, u32[]{:S(2)}) collective-permute-start(f32[4,2,256,128]{3,2,1,0:T(8,128)S(1)} %slice.79), channel_id=1, source_target_pairs={{0,96},{4,100},{8,104},{12,108},{16,112},{20,116},{24,120},{28,124... | collective-permute-start | bytes 3145736 | tf_op jit(solution)/shard_map/ppermute | solution.py:481
  359.1 24.4 %collective-permute-start.23 = (f32[4,2,256,128]{3,2,1,0:T(8,128)S(1)}, f32[4,2,256,128]{3,2,1,0:T(8,128)}, u32[]{:S(2)}, u32[]{:S(2)}) collective-permute-start(f32[4,2,256,128]{3,2,1,0:T(8,128)S(1)} %slice.78), channel_id=1, source_target_pairs={{0,32},{4,36},{8,40},{12,44},{16,48},{20,52},{24,56},{28,60},{32,6... | collective-permute-start | bytes 3145736 | tf_op jit(solution)/shard_map/ppermute | solution.py:480
  363.1 23.7 %collective-permute-start.29 = (f32[4,2,256,128]{3,2,1,0:T(8,128)S(1)}, f32[4,2,256,128]{3,2,1,0:T(8,128)S(1)}, u32[]{:S(2)}, u32[]{:S(2)}) collective-permute-start(f32[4,2,256,128]{3,2,1,0:T(8,128)S(1)} %slice.81), channel_id=1, source_target_pairs={{0,24},{4,28},{8,0},{12,4},{16,8},{20,12},{24,16},{28,20},{32,56},... | collective-permute-start | bytes 3145736 | tf_op jit(solution)/shard_map/ppermute | solution.py:481
  364.5 24.9 %collective-permute-start.27 = (f32[4,2,256,128]{3,2,1,0:T(8,128)S(1)}, f32[4,2,256,128]{3,2,1,0:T(8,128)S(1)}, u32[]{:S(2)}, u32[]{:S(2)}) collective-permute-start(f32[4,2,256,128]{3,2,1,0:T(8,128)S(1)} %slice.80), channel_id=1, source_target_pairs={{0,8},{4,12},{8,16},{12,20},{16,24},{20,28},{24,0},{28,4},{32,40},... | collective-permute-start | bytes 3145736 | tf_op jit(solution)/shard_map/ppermute | solution.py:480
  (22 other events, 400.3 us)
Sparse Core Ops, SparseCore 0:
  116.6 49.0 all-gather.4
  193.7 60.2 all-gather.6

commit v2 on v1

--- a/solution.py
+++ b/solution.py
@@ -420,12 +420,13 @@
     my_x, my_z = my_row // 8, jnp.bitwise_and(my_row // 2, 3)
     z = jnp.bitwise_and(my_col + 4 - step % 4, 3)
     mine = jnp.bitwise_and(my_x + 4 - turns, 3)
-    idle = jnp.where(x < mine, my_col, jnp.bitwise_and(my_col + 1, 3))
+    z_turn = jnp.bitwise_and(my_z + 4 - z, 3)
+    idle = jnp.bitwise_and(my_z + 4 - jnp.where(x < mine, my_col, jnp.bitwise_and(my_col + 1, 3)), 3)
     value = jnp.where(step == 0, my_row, my_col)
     value = jnp.where(line == 8, jnp.bitwise_and(my_col, 1), value)
-    value = jnp.where(line == 7, x, value)
-    value = jnp.where(line < 7, jnp.where(x == mine, z, idle), value)
-    value = jnp.where(line == 1, jnp.bitwise_and(my_z + 4 - z, 3), value)
+    value = jnp.where(line == 7, jnp.bitwise_and(my_x + 4 - x, 3), value)
+    value = jnp.where(line < 7, jnp.where(x == mine, z_turn, idle), value)
+    value = jnp.where(line == 1, z_turn, value)
     return jnp.where(line == 0, jnp.bitwise_and(my_x + 4 - x, 3), value).astype(jnp.int32)
 
 
@@ -482,12 +483,9 @@
     return value, below, first, second, above
 
 
-def gathered(value, axis):
-    if axis == "x":
-        groups = [[x * 8 + rest for x in range(4)] for rest in range(8)]
-    else:
-        groups = [[x * 8 + z * 2 + y for z in range(4)] for x in range(4) for y in range(2)]
-    return lax.all_gather(value, "row", axis_index_groups=groups)
+def short_ring(value, axis, opposite):
+    below, above = ring_near(value, axis)
+    return jnp.stack([value, below, opposite, above])
 
 
 def across(value, pairs, axis):
@@ -555,8 +553,10 @@
 
     lo = ring_z(pair[:, :LOW], lambda core: [2 * core])
     hi = spread_x(pair[:, LOW:])
-    lo, hi = lax.optimization_barrier((lo, hi))
-    return spread_x(lo), ring_z(hi, lambda core: range(4)), jnp.stack([moved, near])
+    panel = jnp.stack([moved, near])
+    opposite = lax.ppermute(panel[:, :512], "row", turn("z", 2))
+    lo, hi, opposite = lax.optimization_barrier((lo, hi, opposite))
+    return spread_x(lo), ring_z(hi, lambda core: range(4)), panel, opposite
 
 
 def shards(contrib, target_rows, diag_shift, pattern):
@@ -579,12 +579,14 @@
     places = [(i, c, ((i // 2) % 4 + c) % 4) for i in range(32) for c in range(4)]
     moved = lax.ppermute(piece, ("row", "col"), [(i * 4 + c, i * 4 + to) for i, c, to in places])
     near = lax.ppermute(piece, ("row", "col"), [(i * 4 + c, (i ^ 1) * 4 + to) for i, c, to in places])
-    corner_lo, corner_hi, pair = corner_columns(piece, moved, near, my_x, my_z, my_y, my_core)
-    lo = gathered(pair[:, :512], "z")
+    corner_lo, corner_hi, pair, opposite = corner_columns(
+        piece, moved, near, my_x, my_z, my_y, my_core
+    )
     corner_lo, corner_hi, main, pair, table = lax.optimization_barrier(
         (corner_lo, corner_hi, main, pair, schur_steps(pos))
     )
-    hi = gathered(pair[:, 512:], "x")
+    lo = short_ring(pair[:, :512], "z", opposite)
+    hi = short_ring(pair[:, 512:], "x", lax.ppermute(pair[:, 512:], "row", turn("x", 2)))
     main = lax.all_to_all(
         main.reshape(128, 128, 128), ("row", "col"), split_axis=0, concat_axis=0, tiled=True
     )

time: 430 us -> 422 us (0.981)
  starting transfers between devices: 56.6 us -> 76.4 us
  waiting for transfers between devices: 114 us -> 95.8 us
  between operations: 14.5 us -> 1.07 us
    ppermute x2 -> x4, starting transfers between devices: 0.1 us -> 16.6 us  [ring_near(): lax.ppermute(value, 'row', turn(axis, -1))]
    ppermute x0 -> x2, starting transfers between devices: none -> 13.7 us  [the longest x1 13.4 us: corner_columns(): opposite = lax.ppermute(panel[:, :512], 'row', turn('z', 2))]
    all_to_all x1, starting transfers between devices: 23.5 us -> 10.1 us  [shards(): lax.all_to_all(main.reshape(128, 128, 128), ('row', 'col'), split_axis=0,...]
    all_to_all x1, waiting for transfers between devices: 13.8 us -> 3.09 us  [shards(): lax.all_to_all(main.reshape(128, 128, 128), ('row', 'col'), split_axis=0,...]
    ppermute x13, waiting for transfers between devices: 49.5 us -> 41.1 us  [moved(): return lax.ppermute(part, both, pairs)]
  transfers between devices with their start and end apart: 33 -> 37, of which waited for: 11 -> 10; matrix products, arithmetic and copies ran while one was open for 5% -> 6% of each run, Pallas kernels for 31% -> 32%
where the time goes in v2:
time: 422 us; the launch traced here: 414 us
  Pallas kernels  180 us (43%)
  waiting for transfers between devices  95.8 us (23%)
  starting transfers between devices  76.4 us (18%)
  blocking collectives  26.6 us (6%)
  other arithmetic  19 us (5%)
  local copies, waits for them, and re-layouts  15.9 us (4%)
    pallas_call x1, Pallas kernels, factor(): pl.pallas_call(factor_kernel, out_shape=(whole, whole), in_specs=[SM, VM,...  101 us
    ppermute x13, waiting for transfers between devices, moved(): return lax.ppermute(part, both, pairs)  41.1 us
    all_to_all x1, blocking collectives, shards(): lax.all_to_all(panel, 'row', split_axis=0, concat_axis=0, tiled=True)  26.6 us
    pallas_call x1, Pallas kernels, schur(): pl.pallas_call(schur_kernel, grid_spec=pltpu.PrefetchScalarGridSpec(num_s...  25.6 us
    ppermute x2, waiting for transfers between devices, ring(): second = lax.ppermute(above[..., half:, :], 'row', turn(axis, -1))  20.6 us
    ppermute x13, starting transfers between devices, moved(): return lax.ppermute(part, both, pairs)  18.9 us
    ppermute x4, starting transfers between devices, ring_near(): lax.ppermute(value, 'row', turn(axis, -1))  16.6 us
    ppermute x1, waiting for transfers between devices, across(): return jnp.stack([value, lax.ppermute(value, axis, pairs)])  15.5 us
  transfers between devices with their start and end apart: 37, of which 10 were waited for; matrix products, arithmetic and copies ran while one was open for 6% of the time, Pallas kernels for 32%

profile of v2, /device:TPU:6, one launch (start us, length us, event | category | flops | bytes accessed | tf_op | source)
XLA Modules:
  0.0 414.3 jit_solution(1974918769087824733)
XLA Ops:
  0.6 14.4 %shard_map.127 = (f32[2304,128]{1,0:T(8,128)}, s32[32,32]{1,0:T(8,128)}, s32[2,256]{1,0:T(2,128)}) custom-call(s32[2]{0:T(128)} %pad_add_fusion.pos_ref, s32[2,256]{1,0:T(2,128)} %t_ref.1, f32[2,256,2048]{2,1,0:T(8,128)} %x_ref.3, f32[2,2,128]{2,1,0:T(2,128)} %bitcast.72), custom_call_target="tpu_custom_call" | custom-call | tf_op jit(solution)/shard_map/pallas_call | solution.py:75
  18.4 26.6 %all_to_all.10 = f32[32,72,128]{2,1,0:T(8,128)S(1)} all-to-all(f32[32,72,128]{2,1,0:T(8,128)} %scatter.4), channel_id=1, replica_groups=mesh['row'=32,'col'=4] {'row'}, dimensions={0} | all-to-all | bytes 2359296 | tf_op jit(solution)/shard_map/all_to_all | solution.py:574
  46.0 7.6 %shard_map.128 = f32[1024,128]{1,0:T(8,128)} custom-call(s32[2]{0:T(128)} %pad_add_fusion.pos_ref, s32[32,96]{1,0:T(8,128)} %convert_bitcast_fusion.marks_ref, s32[2,32]{1,0:T(2,128)} %pattern_ref.3, f32[2304,128]{1,0:T(8,128)} %bitcast.51), custom_call_target="tpu_custom_call" | custom-call | tf_op jit(solution)/shard_map/pallas_call | solution.py:156
  58.2 8.5 %collective-permute-done.5 = f32[1024,128]{1,0:T(8,128)S(1)} collective-permute-done((f32[1024,128]{1,0:T(8,128)}, f32[1024,128]{1,0:T(8,128)S(1)}, u32[]{:S(2)}, u32[]{:S(2)}) %collective-permute-start.5) | collective-permute-done | bytes 524320 | tf_op jit(solution)/shard_map/ppermute | solution.py:581
  76.6 13.4 %collective-permute-start.12 = (f32[2,512,128]{2,1,0:T(8,128)S(1)}, f32[2,512,128]{2,1,0:T(8,128)S(1)}, u32[]{:S(2)}, u32[]{:S(2)}) collective-permute-start(f32[2,512,128]{2,1,0:T(8,128)S(1)} %fusion.2), channel_id=1, source_target_pairs={{0,16},{4,20},{8,24},{12,28},{16,0},{20,4},{24,8},{28,12},{32,48},... | collective-permute-start | bytes 1572872 | tf_op jit(solution)/shard_map/ppermute | solution.py:557
  91.6 14.9 %collective-permute-done.10 = f32[2,640,128]{2,1,0:T(8,128)} collective-permute-done((f32[2,640,128]{2,1,0:T(8,128)S(1)}, f32[2,640,128]{2,1,0:T(8,128)}, u32[]{:S(2)}, u32[]{:S(2)}) %collective-permute-start.10) | collective-permute-done | bytes 655392 | tf_op jit(solution)/shard_map/ppermute | solution.py:533
  109.7 1.8 collective-permute-start.13
  112.2 3.2 collective-permute-start.19
  116.3 26.2 %collective-permute-done.14 = f32[4,2,384,128]{3,2,1,0:T(8,128)} collective-permute-done((f32[4,2,384,128]{3,2,1,0:T(8,128)S(1)}, f32[4,2,384,128]{3,2,1,0:T(8,128)}, u32[]{:S(2)}, u32[]{:S(2)}) %collective-permute-start.14) | collective-permute-done | bytes 1572896 | tf_op jit(solution)/shard_map/ppermute | solution.py:533
  142.6 2.1 slice.82
  144.6 2.2 collective-permute-start.16
  146.9 2.1 slice.81
  150.6 9.5 %shard_map.129 = f32[16384,128]{1,0:T(8,128)} custom-call(s32[2,256]{1,0:T(2,128)} %get-tuple-element.58.slots_ref, f32[2,256,2048]{2,1,0:T(8,128)} %x_ref.3), custom_call_target="tpu_custom_call" | custom-call | flops 10000000000 | bytes 8388608 | tf_op jit(solution)/shard_map/pallas_call | solution.py:108
  160.3 3.2 pad_maximum_fusion.hi_ref
  163.5 3.4 fusion.1.lo_ref
  167.7 3.7 collective-permute-start.21
  171.7 2.0 collective-permute-start.24
  173.7 10.1 %all-to-all-start.1 = ((f32[128,128,128]{2,1,0:T(8,128)}), f32[128,128,128]{2,1,0:T(8,128)}, u32[]{:S(2)}, u32[]{:S(2)}) async-start(f32[128,128,128]{2,1,0:T(8,128)} %bitcast.50), calls=%async_computation.1 | async-start | bytes 16777216 | tf_op jit(solution)/shard_map/all_to_all | solution.py:590
  183.8 100.6 %shard_map.130 = (f32[1024,1024]{1,0:T(8,128)}, f32[1024,1024]{1,0:T(8,128)}) custom-call(s32[2]{0:T(128)} %pad_add_fusion.pos_ref, f32[4,2,384,128]{3,2,1,0:T(8,128)} %fusion.1.lo_ref, f32[4,2,640,128]{3,2,1,0:T(8,128)} %pad_maximum_fusion.hi_ref), custom_call_target="tpu_custom_call" | custom-call | flops 99999997952 | bytes 12582912 | tf_op jit(solution)/shard_map/pallas_call | solution.py:295
  286.6 3.6 pad_maximum_fusion.3.refs_5_
  290.2 3.1 all-to-all-done.1
  293.3 4.7 %collective-permute-start.28 = (f32[4,2,512,128]{3,2,1,0:T(8,128)S(1)}, f32[4,2,512,128]{3,2,1,0:T(8,128)}, u32[]{:S(2)}, u32[]{:S(2)}) collective-permute-start(f32[4,2,512,128]{3,2,1,0:T(8,128)S(1)} %pad_maximum_fusion.2.refs_0_), channel_id=1, source_target_pairs={{0,32},{4,36},{8,40},{12,44},{16,48},{20,52},{24,56},{28,60},{32,6... | collective-permute-start | bytes 6291464 | tf_op jit(solution)/shard_map/ppermute | solution.py:476
  298.0 10.9 %collective-permute-start.34 = (f32[4,2,512,128]{3,2,1,0:T(8,128)}, f32[4,2,512,128]{3,2,1,0:T(8,128)}, u32[]{:S(2)}, u32[]{:S(2)}) collective-permute-start(f32[4,2,512,128]{3,2,1,0:T(8,128)} %pad_maximum_fusion.3.refs_5_), channel_id=1, source_target_pairs={{0,24},{4,28},{8,0},{12,4},{16,8},{20,12},{24,16},{28,20},{32,56},... | collective-permute-start | bytes 6291464 | tf_op jit(solution)/shard_map/ppermute | solution.py:476
  308.9 12.0 %shard_map.131 = (f32[2,4096,128]{2,1,0:T(8,128)}, f32[2,256,256]{2,1,0:T(8,128)}) custom-call(s32[2]{0:T(128)} %pad_add_fusion.pos_ref, s32[32,96]{1,0:T(8,128)} %convert_bitcast_fusion.marks_ref, s32[2,32]{1,0:T(2,128)} %pattern_ref.3, f32[2,2,128]{2,1,0:T(2,128)} %bitcast.73, f32[16384,128]{1,0:T(8,128)} %bitcast.35.x_ref), custom_call_target="tpu_custom_call" | custom-call | flops 1000000 | bytes 4096 | tf_op jit(solution)/shard_map/pallas_call | solution.py:212
  324.0 15.5 %collective-permute-done.26 = f32[2,256,256]{2,1,0:T(8,128)S(1)} collective-permute-done((f32[2,256,256]{2,1,0:T(8,128)S(1)}, f32[2,256,256]{2,1,0:T(8,128)S(1)}, u32[]{:S(2)}, u32[]{:S(2)}) %collective-permute-start.26) | collective-permute-done | bytes 524320 | tf_op jit(solution)/shard_map/ppermute | solution.py:492
  340.5 9.8 %shard_map.132 = (f32[256,1280]{1,0:T(8,128)}, f32[256,1280]{1,0:T(8,128)}) custom-call(s32[2]{0:T(128)} %pad_add_fusion.pos_ref, f32[2,2,256,256]{3,2,1,0:T(8,128)} %pad_maximum_fusion.6.a_ref, f32[1024,1024]{1,0:T(8,128)} %get-tuple-element.69.x_ref, f32[1024,1024]{1,0:T(8,128)} %get-tuple-element.70.head_ref), custom_call_target="tpu_custom_call" | custom-call | flops 1000000 | bytes 4096 | tf_op jit(solution)/shard_map/pallas_call | solution.py:331
  353.1 3.3 collective-permute-start.29
  357.7 3.1 collective-permute-start.35
  362.2 16.4 %collective-permute-done.31.refs_3_ = f32[4,2,256,128]{3,2,1,0:T(8,128)} collective-permute-done((f32[4,2,256,128]{3,2,1,0:T(8,128)S(1)}, f32[4,2,256,128]{3,2,1,0:T(8,128)}, u32[]{:S(2)}, u32[]{:S(2)}) %collective-permute-start.31) | collective-permute-done | bytes 1048608 | tf_op jit(solution)/shard_map/ppermute | solution.py:482
  379.2 4.2 %collective-permute-done.35.refs_8_ = f32[4,2,256,128]{3,2,1,0:T(8,128)S(1)} collective-permute-done((f32[4,2,256,128]{3,2,1,0:T(8,128)S(1)}, f32[4,2,256,128]{3,2,1,0:T(8,128)S(1)}, u32[]{:S(2)}, u32[]{:S(2)}) %collective-permute-start.35) | collective-permute-done | bytes 1048608 | tf_op jit(solution)/shard_map/ppermute | solution.py:482
  383.3 4.9 %collective-permute-done.33.refs_7_ = f32[4,2,256,128]{3,2,1,0:T(8,128)} collective-permute-done((f32[4,2,256,128]{3,2,1,0:T(8,128)S(1)}, f32[4,2,256,128]{3,2,1,0:T(8,128)}, u32[]{:S(2)}, u32[]{:S(2)}) %collective-permute-start.33) | collective-permute-done | bytes 1048608 | tf_op jit(solution)/shard_map/ppermute | solution.py:481
  388.2 25.6 %shard_map.133 = f32[2,4096,128]{2,1,0:T(8,128)} custom-call(s32[160]{0:T(256)} %fusion.5.table_ref, f32[2,4096,128]{2,1,0:T(8,128)} %get-tuple-element.67.front_ref, f32[256,1280]{1,0:T(8,128)} %get-tuple-element.71.kept_ref, f32[256,1280]{1,0:T(8,128)} %copy-done.6, f32[4,2,512,128]{3,2,1,0:T(8,128)} %copy-done, ...), custom_call_target="tpu_custom_call" | custom-call | tf_op jit(solution)/shard_map/pallas_call | solution.py:441
  (130 shorter events, 40.6 us)
Async XLA Ops:
  53.5 13.2 %collective-permute-start.5 = (f32[1024,128]{1,0:T(8,128)}, f32[1024,128]{1,0:T(8,128)S(1)}, u32[]{:S(2)}, u32[]{:S(2)}) collective-permute-start(f32[1024,128]{1,0:T(8,128)} %shard_map.128), channel_id=1, source_target_pairs={{0,4},{1,5},{2,6},{3,7},{4,0},{5,1},{6,2},{7,3},{8,13},{9,14},{10,... | collective-permute-start | bytes 1572872 | tf_op jit(solution)/shard_map/ppermute | solution.py:581
  54.4 13.1 %collective-permute-start.4 = (f32[1024,128]{1,0:T(8,128)}, f32[1024,128]{1,0:T(8,128)S(1)}, u32[]{:S(2)}, u32[]{:S(2)}) collective-permute-start(f32[1024,128]{1,0:T(8,128)} %shard_map.128), channel_id=1, source_target_pairs={{0,0},{1,1},{2,2},{3,3},{4,4},{5,5},{6,6},{7,7},{8,9},{9,10},{10,1... | collective-permute-start | bytes 1572872 | tf_op jit(solution)/shard_map/ppermute | solution.py:580
  56.1 11.4 %collective-permute-start.3 = (f32[1024,128]{1,0:T(8,128)}, f32[1024,128]{1,0:T(8,128)S(1)}, u32[]{:S(2)}, u32[]{:S(2)}) collective-permute-start(f32[1024,128]{1,0:T(8,128)} %shard_map.128), channel_id=1, source_target_pairs={{0,6},{4,0},{8,14},{12,8},{16,22},{20,16},{24,30},{28,24},{64,71},... | collective-permute-start | bytes 1572872 | tf_op jit(solution)/shard_map/ppermute | solution.py:517
  56.8 10.7 %collective-permute-start.2 = (f32[1024,128]{1,0:T(8,128)}, f32[1024,128]{1,0:T(8,128)S(1)}, u32[]{:S(2)}, u32[]{:S(2)}) collective-permute-start(f32[1024,128]{1,0:T(8,128)} %shard_map.128), channel_id=1, source_target_pairs={{0,2},{4,6},{8,10},{12,14},{16,18},{20,22},{24,26},{28,30},{64,67}... | collective-permute-start | bytes 1572872 | tf_op jit(solution)/shard_map/ppermute | solution.py:517
  70.8 35.7 %collective-permute-start.10 = (f32[2,640,128]{2,1,0:T(8,128)S(1)}, f32[2,640,128]{2,1,0:T(8,128)}, u32[]{:S(2)}, u32[]{:S(2)}) collective-permute-start(f32[2,640,128]{2,1,0:T(8,128)S(1)} %pad_maximum_fusion.7), channel_id=1, source_target_pairs={{0,96},{65,33},{4,100},{69,37},{2,98},{67,35},{6,102},{71,39},{8,1... | collective-permute-start | bytes 1966088 | tf_op jit(solution)/shard_map/ppermute | solution.py:533
  72.1 34.4 %collective-permute-start.9 = (f32[2,640,128]{2,1,0:T(8,128)S(1)}, f32[2,640,128]{2,1,0:T(8,128)}, u32[]{:S(2)}, u32[]{:S(2)}) collective-permute-start(f32[2,640,128]{2,1,0:T(8,128)S(1)} %pad_maximum_fusion.7), channel_id=1, source_target_pairs={{0,32},{65,97},{4,36},{69,101},{2,34},{67,99},{6,38},{71,103},{8,4... | collective-permute-start | bytes 1966088 | tf_op jit(solution)/shard_map/ppermute | solution.py:533
  73.6 32.8 %collective-permute-start.11 = (f32[2,640,128]{2,1,0:T(8,128)S(1)}, f32[2,640,128]{2,1,0:T(8,128)}, u32[]{:S(2)}, u32[]{:S(2)}) collective-permute-start(f32[2,640,128]{2,1,0:T(8,128)S(1)} %pad_maximum_fusion.7), channel_id=1, source_target_pairs={{0,64},{65,1},{4,68},{69,5},{2,66},{67,3},{6,70},{71,7},{8,72},{73... | collective-permute-start | bytes 1966088 | tf_op jit(solution)/shard_map/ppermute | solution.py:533
  75.1 15.0 %collective-permute-start.8 = (f32[2,384,128]{2,1,0:T(8,128)}, f32[2,384,128]{2,1,0:T(8,128)}, u32[]{:S(2)}, u32[]{:S(2)}) collective-permute-start(f32[2,384,128]{2,1,0:T(8,128)} %pad_maximum_fusion.9), channel_id=1, source_target_pairs={{0,24},{65,89},{4,28},{69,93},{2,26},{67,91},{6,30},{71,95},{8,0},... | collective-permute-start | bytes 1179656 | tf_op jit(solution)/shard_map/ppermute | solution.py:550
  76.6 31.1 %collective-permute-start.12 = (f32[2,512,128]{2,1,0:T(8,128)S(1)}, f32[2,512,128]{2,1,0:T(8,128)S(1)}, u32[]{:S(2)}, u32[]{:S(2)}) collective-permute-start(f32[2,512,128]{2,1,0:T(8,128)S(1)} %fusion.2), channel_id=1, source_target_pairs={{0,16},{4,20},{8,24},{12,28},{16,0},{20,4},{24,8},{28,12},{32,48},... | collective-permute-start | bytes 1572872 | tf_op jit(solution)/shard_map/ppermute | solution.py:557
  108.4 34.1 %collective-permute-start.14 = (f32[4,2,384,128]{3,2,1,0:T(8,128)S(1)}, f32[4,2,384,128]{3,2,1,0:T(8,128)}, u32[]{:S(2)}, u32[]{:S(2)}) collective-permute-start(f32[4,2,384,128]{3,2,1,0:T(8,128)S(1)} %pad_maximum_fusion.4), channel_id=1, source_target_pairs={{0,96},{65,33},{4,100},{69,37},{2,98},{67,35},{6,102},{71,39},{8,1... | collective-permute-start | bytes 4718600 | tf_op jit(solution)/shard_map/ppermute | solution.py:533
  109.7 37.1 %collective-permute-start.13 = (f32[4,2,384,128]{3,2,1,0:T(8,128)S(1)}, f32[4,2,384,128]{3,2,1,0:T(8,128)}, u32[]{:S(2)}, u32[]{:S(2)}) collective-permute-start(f32[4,2,384,128]{3,2,1,0:T(8,128)S(1)} %pad_maximum_fusion.4), channel_id=1, source_target_pairs={{0,32},{65,97},{4,36},{69,101},{2,34},{67,99},{6,38},{71,103},{8,4... | collective-permute-start | bytes 4718600 | tf_op jit(solution)/shard_map/ppermute | solution.py:533
  112.2 48.0 %collective-permute-start.19 = (f32[2,640,128]{2,1,0:T(8,128)S(1)}, f32[2,640,128]{2,1,0:T(8,128)}, u32[]{:S(2)}, u32[]{:S(2)}) collective-permute-start(f32[2,640,128]{2,1,0:T(8,128)S(1)} %select_select_fusion), channel_id=1, source_target_pairs={{0,24},{32,56},{64,88},{96,120},{1,25},{33,57},{65,89},{97,121},{4... | collective-permute-start | bytes 1966088 | tf_op jit(solution)/shard_map/ppermute | solution.py:550
  115.5 44.8 %collective-permute-start.18 = (f32[2,640,128]{2,1,0:T(8,128)S(1)}, f32[2,640,128]{2,1,0:T(8,128)}, u32[]{:S(2)}, u32[]{:S(2)}) collective-permute-start(f32[2,640,128]{2,1,0:T(8,128)S(1)} %select_select_fusion), channel_id=1, source_target_pairs={{0,16},{32,48},{64,80},{96,112},{1,17},{33,49},{65,81},{97,113},{4... | collective-permute-start | bytes 1966088 | tf_op jit(solution)/shard_map/ppermute | solution.py:550
  115.5 44.8 %collective-permute-start.17 = (f32[2,640,128]{2,1,0:T(8,128)S(1)}, f32[2,640,128]{2,1,0:T(8,128)}, u32[]{:S(2)}, u32[]{:S(2)}) collective-permute-start(f32[2,640,128]{2,1,0:T(8,128)S(1)} %select_select_fusion), channel_id=1, source_target_pairs={{0,8},{32,40},{64,72},{96,104},{1,9},{33,41},{65,73},{97,105},{4,1... | collective-permute-start | bytes 1966088 | tf_op jit(solution)/shard_map/ppermute | solution.py:550
  144.6 18.8 %collective-permute-start.16 = (f32[4,2,192,128]{3,2,1,0:T(8,128)}, f32[4,2,192,128]{3,2,1,0:T(8,128)}, u32[]{:S(2)}, u32[]{:S(2)}) collective-permute-start(f32[4,2,192,128]{3,2,1,0:T(8,128)} %slice.82), channel_id=1, source_target_pairs={{96,64},{33,1},{100,68},{37,5},{98,66},{35,3},{102,70},{39,7},{104... | collective-permute-start | bytes 2359304 | tf_op jit(solution)/shard_map/ppermute | solution.py:533
  149.0 14.5 %collective-permute-start.15 = (f32[4,2,192,128]{3,2,1,0:T(8,128)}, f32[4,2,192,128]{3,2,1,0:T(8,128)}, u32[]{:S(2)}, u32[]{:S(2)}) collective-permute-start(f32[4,2,192,128]{3,2,1,0:T(8,128)} %slice.81), channel_id=1, source_target_pairs={{32,64},{97,1},{36,68},{101,5},{34,66},{99,3},{38,70},{103,7},{40,... | collective-permute-start | bytes 2359304 | tf_op jit(solution)/shard_map/ppermute | solution.py:533
  167.7 116.6 %collective-permute-start.20 = (f32[2,512,128]{2,1,0:T(8,128)S(1)}, f32[2,512,128]{2,1,0:T(8,128)}, u32[]{:S(2)}, u32[]{:S(2)}) collective-permute-start(f32[2,512,128]{2,1,0:T(8,128)S(1)} %get-tuple-element.80), channel_id=1, source_target_pairs={{0,8},{4,12},{8,16},{12,20},{16,24},{20,28},{24,0},{28,4},{32,40},... | collective-permute-start | bytes 1572872 | tf_op jit(solution)/shard_map/ppermute | solution.py:476
  167.7 116.6 %collective-permute-start.21 = (f32[2,512,128]{2,1,0:T(8,128)S(1)}, f32[2,512,128]{2,1,0:T(8,128)S(1)}, u32[]{:S(2)}, u32[]{:S(2)}) collective-permute-start(f32[2,512,128]{2,1,0:T(8,128)S(1)} %get-tuple-element.80), channel_id=1, source_target_pairs={{0,24},{4,28},{8,0},{12,4},{16,8},{20,12},{24,16},{28,20},{32,56},... | collective-permute-start | bytes 1572872 | tf_op jit(solution)/shard_map/ppermute | solution.py:476
  171.4 115.1 %collective-permute-start.23 = (f32[2,512,128]{2,1,0:T(8,128)}, f32[2,512,128]{2,1,0:T(8,128)}, u32[]{:S(2)}, u32[]{:S(2)}) collective-permute-start(f32[2,512,128]{2,1,0:T(8,128)} %get-tuple-element.79), channel_id=1, source_target_pairs={{0,64},{4,68},{8,72},{12,76},{16,80},{20,84},{24,88},{28,92},{32,9... | collective-permute-start | bytes 1572872 | tf_op jit(solution)/shard_map/ppermute | solution.py:589
  171.7 114.9 %collective-permute-start.22 = (f32[2,512,128]{2,1,0:T(8,128)}, f32[2,512,128]{2,1,0:T(8,128)}, u32[]{:S(2)}, u32[]{:S(2)}) collective-permute-start(f32[2,512,128]{2,1,0:T(8,128)} %get-tuple-element.79), channel_id=1, source_target_pairs={{0,32},{4,36},{8,40},{12,44},{16,48},{20,52},{24,56},{28,60},{32,6... | collective-permute-start | bytes 1572872 | tf_op jit(solution)/shard_map/ppermute | solution.py:476
  171.7 114.9 %collective-permute-start.24 = (f32[2,512,128]{2,1,0:T(8,128)}, f32[2,512,128]{2,1,0:T(8,128)}, u32[]{:S(2)}, u32[]{:S(2)}) collective-permute-start(f32[2,512,128]{2,1,0:T(8,128)} %get-tuple-element.79), channel_id=1, source_target_pairs={{0,96},{4,100},{8,104},{12,108},{16,112},{20,116},{24,120},{28,124... | collective-permute-start | bytes 1572872 | tf_op jit(solution)/shard_map/ppermute | solution.py:476
  173.7 119.6 %all-to-all-start.1 = ((f32[128,128,128]{2,1,0:T(8,128)}), f32[128,128,128]{2,1,0:T(8,128)}, u32[]{:S(2)}, u32[]{:S(2)}) async-start(f32[128,128,128]{2,1,0:T(8,128)} %bitcast.50), calls=%async_computation.1 | async-start | bytes 16777216 | tf_op jit(solution)/shard_map/all_to_all | solution.py:590
  293.3 57.1 %collective-permute-start.30 = (f32[4,2,512,128]{3,2,1,0:T(8,128)S(1)}, f32[4,2,512,128]{3,2,1,0:T(8,128)}, u32[]{:S(2)}, u32[]{:S(2)}) collective-permute-start(f32[4,2,512,128]{3,2,1,0:T(8,128)S(1)} %pad_maximum_fusion.2.refs_0_), channel_id=1, source_target_pairs={{0,96},{4,100},{8,104},{12,108},{16,112},{20,116},{24,120},{28,124... | collective-permute-start | bytes 6291464 | tf_op jit(solution)/shard_map/ppermute | solution.py:476
  293.3 58.4 %collective-permute-start.28 = (f32[4,2,512,128]{3,2,1,0:T(8,128)S(1)}, f32[4,2,512,128]{3,2,1,0:T(8,128)}, u32[]{:S(2)}, u32[]{:S(2)}) collective-permute-start(f32[4,2,512,128]{3,2,1,0:T(8,128)S(1)} %pad_maximum_fusion.2.refs_0_), channel_id=1, source_target_pairs={{0,32},{4,36},{8,40},{12,44},{16,48},{20,52},{24,56},{28,60},{32,6... | collective-permute-start | bytes 6291464 | tf_op jit(solution)/shard_map/ppermute | solution.py:476
  298.0 58.3 %collective-permute-start.34 = (f32[4,2,512,128]{3,2,1,0:T(8,128)}, f32[4,2,512,128]{3,2,1,0:T(8,128)}, u32[]{:S(2)}, u32[]{:S(2)}) collective-permute-start(f32[4,2,512,128]{3,2,1,0:T(8,128)} %pad_maximum_fusion.3.refs_5_), channel_id=1, source_target_pairs={{0,24},{4,28},{8,0},{12,4},{16,8},{20,12},{24,16},{28,20},{32,56},... | collective-permute-start | bytes 6291464 | tf_op jit(solution)/shard_map/ppermute | solution.py:476
  308.9 51.9 %collective-permute-start.32 = (f32[4,2,512,128]{3,2,1,0:T(8,128)}, f32[4,2,512,128]{3,2,1,0:T(8,128)}, u32[]{:S(2)}, u32[]{:S(2)}) collective-permute-start(f32[4,2,512,128]{3,2,1,0:T(8,128)} %pad_maximum_fusion.3.refs_5_), channel_id=1, source_target_pairs={{0,8},{4,12},{8,16},{12,20},{16,24},{20,28},{24,0},{28,4},{32,40},... | collective-permute-start | bytes 6291464 | tf_op jit(solution)/shard_map/ppermute | solution.py:476
  323.7 15.8 %collective-permute-start.26 = (f32[2,256,256]{2,1,0:T(8,128)S(1)}, f32[2,256,256]{2,1,0:T(8,128)S(1)}, u32[]{:S(2)}, u32[]{:S(2)}) collective-permute-start(f32[2,256,256]{2,1,0:T(8,128)S(1)} %get-tuple-element.82), channel_id=1, source_target_pairs={{0,2},{2,0},{1,3},{3,1},{4,6},{6,4},{5,7},{7,5},{8,10},{10,8},{9,1... | collective-permute-start | bytes 1572872 | tf_op jit(solution)/shard_map/ppermute | solution.py:492
  350.4 11.8 %collective-permute-start.27 = (f32[256,1280]{1,0:T(8,128)}, f32[256,1280]{1,0:T(8,128)S(1)}, u32[]{:S(2)}, u32[]{:S(2)}) collective-permute-start(f32[256,1280]{1,0:T(8,128)} %get-tuple-element.72), channel_id=1, source_target_pairs={{0,1},{1,0},{2,3},{3,2},{4,5},{5,4},{6,7},{7,6},{8,9},{9,8},{10,11... | collective-permute-start | bytes 3932168 | tf_op jit(solution)/shard_map/ppermute | solution.py:600
  351.7 27.0 %collective-permute-start.31 = (f32[4,2,256,128]{3,2,1,0:T(8,128)S(1)}, f32[4,2,256,128]{3,2,1,0:T(8,128)}, u32[]{:S(2)}, u32[]{:S(2)}) collective-permute-start(f32[4,2,256,128]{3,2,1,0:T(8,128)S(1)} %slice.84), channel_id=1, source_target_pairs={{0,96},{4,100},{8,104},{12,108},{16,112},{20,116},{24,120},{28,124... | collective-permute-start | bytes 3145736 | tf_op jit(solution)/shard_map/ppermute | solution.py:482
  353.1 26.1 %collective-permute-start.29 = (f32[4,2,256,128]{3,2,1,0:T(8,128)S(1)}, f32[4,2,256,128]{3,2,1,0:T(8,128)S(1)}, u32[]{:S(2)}, u32[]{:S(2)}) collective-permute-start(f32[4,2,256,128]{3,2,1,0:T(8,128)S(1)} %slice.83), channel_id=1, source_target_pairs={{0,32},{4,36},{8,40},{12,44},{16,48},{20,52},{24,56},{28,60},{32,6... | collective-permute-start | bytes 3145736 | tf_op jit(solution)/shard_map/ppermute | solution.py:481
  357.7 25.7 %collective-permute-start.35 = (f32[4,2,256,128]{3,2,1,0:T(8,128)S(1)}, f32[4,2,256,128]{3,2,1,0:T(8,128)S(1)}, u32[]{:S(2)}, u32[]{:S(2)}) collective-permute-start(f32[4,2,256,128]{3,2,1,0:T(8,128)S(1)} %slice.86), channel_id=1, source_target_pairs={{0,24},{4,28},{8,0},{12,4},{16,8},{20,12},{24,16},{28,20},{32,56},... | collective-permute-start | bytes 3145736 | tf_op jit(solution)/shard_map/ppermute | solution.py:482
  362.1 26.1 %collective-permute-start.33 = (f32[4,2,256,128]{3,2,1,0:T(8,128)S(1)}, f32[4,2,256,128]{3,2,1,0:T(8,128)}, u32[]{:S(2)}, u32[]{:S(2)}) collective-permute-start(f32[4,2,256,128]{3,2,1,0:T(8,128)S(1)} %slice.85), channel_id=1, source_target_pairs={{0,8},{4,12},{8,16},{12,20},{16,24},{20,28},{24,0},{28,4},{32,40},... | collective-permute-start | bytes 3145736 | tf_op jit(solution)/shard_map/ppermute | solution.py:481
  (28 other events, 434.3 us)
